TPU v7x, 128 devices: a whole 4x4x4 slice. The times are simulated.
128 devices in a mesh: row: 16 (over z, x_hi, core), col: 8 (over y, x_lo).
Axes of the slice: x: 4 (x_hi: 2, x_lo: 2; x = x_hi * 2 + x_lo), y: 4, z: 4, core: 2. Of those that a mesh axis runs over, the one named last changes fastest.
Arguments:
- matrix: bfloat16 [8192, 8192], P('row', 'col'), may hold values from -6 to 6
- factors: float32 [8192, 8192], P('row', 'col')
- inverse: bfloat16 [64, 128, 128], P('col'), may hold values from -0.007171631 to 0.007171631
- pattern: int32 [64, 64], P('row', 'col'), may hold values from 0 to 1, as said below
- dropped: int32 [64, 64], P('row', 'col'), may hold values from 0 to 1, as said below
Outputs:
- factors_out: float32 [8192, 8192], P('row', 'col')
Inputs may be any that keep to these rules, and one draw needn't show every extreme that they name: Block (I, J) can be in the pattern only where I - J is 0, 1, -1, 4, -4, 32 or -32; the blocks with I - J of 0, 1, -1, 4 and -4 are always in it. In each device's region of 4 block rows by 8 block columns, every block column holds at most 3 pattern blocks (exactly 3 in some columns), and every block row at most 2 pattern blocks below the block diagonal (exactly 2 in some rows). `dropped`: dropped blocks lie in the pattern and off the block diagonal.
All inputs are finite; a program needn't handle non-finite values.
Results may differ from a plain program's by a relative error of at most 0.00083.
Values may be sent and summed in bfloat16 or wider, within the bound.
No kernel may reach another device: no remote copies, remote signals or barrier semaphores. Data moves between devices by JAX's collectives and lax.ppermute only.
A program may use at most 128 MiB of HBM per device.

v0:
```python
import functools

import jax
import jax.numpy as jnp
import numpy as np
from jax import lax
from jax.experimental import pallas as pl
from jax.experimental.pallas import tpu as pltpu
from jax.sharding import PartitionSpec as P

BS = 128
F32 = jnp.float32
BF16 = jnp.bfloat16

DIAG, X, OFF = 0, 4, 5
HELD = 9


def role():
    r, c = lax.axis_index("row"), lax.axis_index("col")
    odd = lax.rem(r, 2)
    home = lax.div(r, 2)
    late = r >= 8
    is_odd = odd == 1
    even = odd == 0
    is_d = c == home
    is_n = jnp.where(is_odd, c == home + 1, c == home - 1)
    is_f = jnp.where(late, c == home - 4, c == home + 4)
    lower = (is_d & is_odd) | (is_n & even) | (is_f & late)
    held = is_d | is_n | is_f
    return dict(
        even=even,
        top=r == 0,
        d=is_d,
        d_even=is_d & even,
        d_odd=is_d & is_odd,
        d_late=is_d & late,
        d_early=is_d & jnp.logical_not(late),
        n_even=is_n & even,
        n_odd=is_n & is_odd,
        f=is_f,
        f_late=is_f & late,
        f_early=is_f & jnp.logical_not(late),
        near=is_d | is_n,
        any=held,
        lower=lower,
        near_lower=lower & jnp.logical_not(is_f),
        upper=held & jnp.logical_not(lower),
        near_upper=held & jnp.logical_not(lower) & jnp.logical_not(is_f),
        first=4 * odd,
        off=jnp.where(is_f, 4 * odd, 4 * (1 - odd)),
        x_row=jnp.where(is_odd, jnp.where(is_d, 0, 3), jnp.where(is_d, 3, 0)),
        x_col=jnp.where(is_odd, jnp.where(is_d, 3, 0), jnp.where(is_d, 4, 7)),
    )


def spot(w, slot):
    if slot == X:
        return w["x_row"], w["x_col"]
    if slot < X:
        return slot, w["first"] + slot
    return slot - OFF, w["off"] + slot - OFF


def block(ref, i, c):
    return ref.at[pl.ds(pl.multiple_of(i * BS, BS), BS), pl.ds(pl.multiple_of(c * BS, BS), BS)]


def dot(a, b):
    return jnp.dot(a, b, preferred_element_type=F32)


class Copies:
    def __init__(self, sem):
        self.sem, self.todo = sem, []

    def add(self, when, src, dst):
        self.todo.append((when, src, dst))

    def run(self, start):
        i = 0
        while i < len(self.todo):
            when = self.todo[i][0]
            j = i
            while j < len(self.todo) and self.todo[j][0] is when:
                j += 1
            some = self.todo[i:j]

            def act(some=some):
                for _, src, dst in some:
                    copy = pltpu.make_async_copy(src, dst, self.sem)
                    copy.start() if start else copy.wait()

            if when is None:
                act()
            else:
                pl.when(when)(act)
            i = j


def member(table, place):
    return (table[place] == 1).astype(F32)


def cut_kernel(pattern, factors, sa, sb, sc, sd, held, table, sem, table_sem):
    w = role()

    @pl.when(w["any"])
    def _():
        get_table = pltpu.make_async_copy(pattern, table, table_sem)
        get_table.start()
        blocks = Copies(sem)
        for s in range(HELD):
            when = w["d"] if s < X else w["near"] if s == X else None
            blocks.add(when, block(factors, *spot(w, s)), held.at[s])
        blocks.run(True)
        get_table.wait()
        blocks.run(False)

        def masked(s):
            value = held[s] * member(table, spot(w, s))
            held[s] = value
            return value.astype(BF16)

        @pl.when(w["d"])
        def _():
            for j in range(4):
                value = masked(DIAG + j)
                sc[j] = value

                @pl.when(w["even"])
                def _():
                    sb[j] = value

                @pl.when(w["d_odd"])
                def _():
                    sa[j] = value

        @pl.when(w["f_early"])
        def _():
            for j in range(4):
                sd[j] = masked(OFF + j)

        @pl.when(w["f_late"])
        def _():
            for j in range(4):
                sc[j] = masked(OFF + j)

        @pl.when(w["d_even"] | w["n_odd"])
        def _():
            for j in range(4):
                sa[j] = masked(OFF + j)
            sa[4] = masked(X)

        @pl.when(w["n_even"])
        def _():
            for j in range(4):
                sb[j] = masked(OFF + j)
            sb[4] = masked(X)

        @pl.when(w["d_odd"])
        def _():
            for j in range(4):
                masked(OFF + j)
            masked(X)


def stage_kernel(pattern, dropped, factors, matrix, inverse, held,
                 out, base, base2, upper_b, a_low, left1, inv, keep,
                 zeros, f, a, done, table, drops, sems):
    w = role()
    zeros[...] = jnp.zeros_like(zeros)
    rows = zeros.shape[0]
    fill = Copies(sems.at[0])
    for k in range(out.shape[0] // rows):
        fill.add(None, zeros, out.at[pl.ds(k * rows, rows)])
    tables = Copies(sems.at[1])
    tables.add(None, pattern, table)
    tables.add(None, dropped, drops)
    blocks = Copies(sems.at[2])
    right = [(j, w["first"] + j + 1) for j in range(3)]
    left = [(j + 1, w["first"] + j) for j in range(3)]
    for k, place in enumerate(right + left):
        blocks.add(w["d"], block(factors, *place), f.at[k])
    for s in range(X):
        blocks.add(w["d"], block(matrix, *spot(w, s)), a.at[s])
    for k, place in enumerate(right + left):
        blocks.add(w["d"], block(matrix, *place), a.at[HELD + k])
    blocks.add(w["near"], block(matrix, *spot(w, X)), a.at[X])
    for s in range(OFF, HELD):
        blocks.add(None, block(matrix, *spot(w, s)), a.at[s])
    blocks.add(None, inverse, inv)

    @pl.when(w["any"])
    def _():
        tables.run(True)
        blocks.run(True)

    fill.run(True)

    @pl.when(w["any"])
    def _():
        tables.run(False)
        blocks.run(False)

        def kept(place):
            return (1 - drops[place]).astype(F32)

        def upper(old, a_block, place):
            m = member(table, place)
            a_block = a_block.astype(F32)
            one = old + (a_block - old) * m
            return one, (one + (a_block - one) * m) * kept(place)

        @pl.when(w["upper"])
        def _():
            for s in range(X, HELD):

                def act(s=s):
                    one, two = upper(held[s], a[s], spot(w, s))
                    upper_b[s - X] = one.astype(BF16)
                    done[s - X] = two

                act() if s > X else pl.when(w["near_upper"])(act)

        @pl.when(w["lower"])
        def _():
            for s in range(X, HELD):

                def act(s=s):
                    place = spot(w, s)
                    a_low[s - X] = (a[s].astype(F32) * member(table, place)).astype(BF16)
                    keep[s - X] = jnp.full(keep.shape[1:], kept(place))

                act() if s > X else pl.when(w["near_lower"])(act)

        @pl.when(w["d"])
        def _():
            base[0] = a[0].astype(F32)
            base2[0] = a[0].astype(F32)
            for j in range(3):
                old_u = f[j] * member(table, right[j])
                one_u, two_u = upper(old_u, a[HELD + j], right[j])
                done[5 + j] = two_u
                m = member(table, left[j])
                old = f[3 + j] * m
                old_b = old.astype(BF16)
                a_block = a[HELD + 3 + j].astype(F32) * m
                residual = a_block - dot(old_b, held[DIAG + j].astype(BF16)) * m
                one = old + dot(residual.astype(BF16), inv[w["first"] + j]) * m
                left1[j] = one
                a_low[5 + j] = a_block.astype(BF16)
                keep[5 + j] = jnp.full(keep.shape[1:], kept(left[j]))
                a_diag = a[j + 1].astype(F32)
                base[j + 1] = a_diag - dot(old_b, old_u.astype(BF16))
                base2[j + 1] = a_diag - dot(one.astype(BF16), one_u.astype(BF16))

    fill.run(False)
    finished = Copies(sems.at[3])
    for s in range(OFF, HELD):
        finished.add(w["upper"], done.at[s - X], block(out, *spot(w, s)))
    finished.add(w["near_upper"], done.at[0], block(out, *spot(w, X)))
    for j in range(3):
        finished.add(w["d"], done.at[5 + j], block(out, *right[j]))
    finished.run(True)
    finished.run(False)


def diagonal(w, sums, l_near, l_x, ra, rc, rd):
    def at(j, with_near, with_far):
        total = sums[j]
        if with_near:
            total = total - dot(l_near(j), ra[j])
        if with_near and j == 0:
            total = total - dot(l_x(), ra[4])
        if with_far:
            total = total - dot(rc[j], rd[j])
        return total

    return at


def lower_step(old, a_block, u, inv_block):
    residual = a_block.astype(F32) - dot(old.astype(BF16), u)
    return old + dot(residual.astype(BF16), inv_block)


def each_diagonal(w, emit, sums, own, rb, ra, rc, rd):
    for parity, l_near, l_x in (
        ("d_even", lambda j: rb[j], lambda: rb[4]),
        ("d_odd", lambda j: own[OFF + j].astype(BF16), lambda: own[X].astype(BF16)),
    ):
        at = diagonal(w, sums, l_near, l_x, ra, rc, rd)
        for near, far in ((False, False), (True, False), (True, True)):
            if not near and parity == "d_odd":
                continue
            when = w["d_late"] if far else w["d_early"] & (w["top"] != near)

            @pl.when(w[parity] & when)
            def _():
                for j in range(4):
                    emit(j, at(j, near, far))


def middle_kernel(held, base, upper_b, a_low, inv, ra, rb, rc, rd,
                  sa, sb, sc, sd, diag1, low1):
    w = role()

    def emit(j, total):
        old = held[DIAG + j]
        one = old + (total - old)
        diag1[j] = one
        value = one.astype(BF16)

        @pl.when(w["even"])
        def _():
            sb[j] = value

        @pl.when(w["d_odd"])
        def _():
            sa[j] = value

        @pl.when(w["d_early"])
        def _():
            sc[j] = value

    each_diagonal(w, emit, base, held, rb, ra, rc, rd)

    @pl.when(w["d_even"] | w["n_odd"])
    def _():
        for j in range(4):
            sa[j] = upper_b[1 + j]
        sa[4] = upper_b[0]

    @pl.when(w["f_early"])
    def _():
        for j in range(4):
            sd[j] = upper_b[1 + j]

    def lower(dst, u, j, s):
        one = lower_step(held[s], a_low[s - X], u[j], inv[w["off"] + j])
        low1[s - X] = one
        dst[s - OFF if s > X else 4] = one.astype(BF16)

    @pl.when(w["n_even"])
    def _():
        for j in range(4):
            lower(sb, ra, j, OFF + j)
        lower(sb, ra, 3, X)

    @pl.when(w["f_late"])
    def _():
        for j in range(4):
            lower(sc, rc, j, OFF + j)


def between_kernel(held, diag1, left1, a_low, inv, keep, rb, out_in, out, low1, done, sem):
    del out_in
    w = role()

    @pl.when(w["d"])
    def _():
        writes = Copies(sem)
        for j in range(3):
            u = diag1[j].astype(BF16)
            two = lower_step(left1[j], a_low[5 + j], u, inv[w["first"] + j])
            done[j] = two * keep[5 + j, 0:1, :]
            writes.add(None, done.at[j], block(out, j + 1, w["first"] + j))
        writes.run(True)

        @pl.when(w["d_odd"])
        def _():
            for j in range(4):
                low1[1 + j] = lower_step(held[OFF + j], a_low[1 + j], rb[j], inv[w["off"] + j])
            low1[0] = lower_step(held[X], a_low[0], rb[3], inv[w["off"] + 3])

        writes.run(False)


def last_kernel(diag1, base2, low1, low1_d, a_low, inv, keep, ra, rb, rc, rd, out_in,
                out, done, sem):
    del out_in
    w = role()
    writes = Copies(sem)
    for j in range(4):
        writes.add(w["d"], done.at[j], block(out, *spot(w, j)))
    for s in range(OFF, HELD):
        writes.add(w["lower"], done.at[s], block(out, *spot(w, s)))
    writes.add(w["near_lower"], done.at[X], block(out, *spot(w, X)))

    class Own:
        def __getitem__(self, s):
            return low1_d[s - X]

    def emit(j, total):
        old = diag1[j]
        done[DIAG + j] = old + (total - old)

    each_diagonal(w, emit, base2, Own(), rb, ra, rc, rd)

    def lower(old, u, j, s):
        two = lower_step(old[s - X], a_low[s - X], u[j], inv[w["off"] + j])
        done[s] = two * keep[s - X, 0:1, :]

    for name, old, u in (("d_odd", low1_d, rb), ("n_even", low1, ra), ("f_late", low1, rc)):

        @pl.when(w[name])
        def _():
            for j in range(4):
                lower(old, u, j, OFF + j)
            if name != "f_late":
                lower(old, u, 3, X)

    writes.run(True)
    writes.run(False)


def matched(cost):
    n = len(cost)
    u, v = np.zeros(n + 1), np.zeros(n + 1)
    owner = np.zeros(n + 1, int)
    for i in range(1, n + 1):
        owner[0], j0 = i, 0
        best = np.full(n + 1, np.inf)
        back = np.zeros(n + 1, int)
        used = np.zeros(n + 1, bool)
        while owner[j0]:
            used[j0] = True
            i0 = owner[j0]
            slack = cost[i0 - 1] - u[i0] - v[1:]
            better = ~used[1:] & (slack < best[1:])
            best[1:][better] = slack[better]
            back[1:][better] = j0
            j1 = int(np.argmin(np.where(used, np.inf, best)))
            delta = best[j1]
            u[owner[used]] += delta
            v[used] -= delta
            best[~used] -= delta
            j0 = j1
        while j0:
            owner[j0] = owner[back[j0]]
            j0 = back[j0]
    return {int(owner[j]) - 1: j - 1 for j in range(1, n + 1)}


def distance(a, b):
    def chip(i):
        r, c = divmod(i, 8)
        return ((r // 2) % 2) * 2 + c % 2, c // 2, r // 4

    return sum(min(abs(p - q), 4 - abs(p - q)) for p, q in zip(chip(a), chip(b)))


def whole(pairs, busy):
    sends, takes = {a for a, _ in pairs}, {b for _, b in pairs}
    free_a = [i for i in range(128) if i not in sends]
    free_b = [i for i in range(128) if i not in takes]

    def price(a, b):
        if a == b:
            return 1e6
        far = distance(a, b)
        return (2 + far if far else 1) ** 2 * sum(10 if i in busy else 1 for i in (a, b))

    pick = matched(np.array([[price(a, b) for b in free_b] for a in free_a], float))
    return list(pairs) + [(a, free_b[pick[i]]) for i, a in enumerate(free_a)]


def routes():
    def at(r, c):
        return r * 8 + c

    diag = [at(r, r // 2) for r in range(16)]
    near = {r: at(r, r // 2 + (1 if r % 2 else -1)) for r in range(1, 15)}
    far = [at(r, r // 2 + (4 if r < 8 else -4)) for r in range(16)]
    busy = {*diag, *near.values(), *far}
    pair = [(diag[r], diag[r + 1]) for r in range(0, 16, 2)]
    a = pair + [(diag[r], near[r + 1]) for r in range(1, 14, 2)]
    a += [(near[r], diag[r + 1]) for r in range(1, 14, 2)]
    b = pair + [(near[r], diag[r]) for r in range(2, 15, 2)]
    c, d = [], []
    for r in range(8):
        ring = [diag[r], far[r + 8], diag[r + 8], far[r]]
        c += list(zip(ring, ring[1:] + ring[:1]))
        d += [(far[r], diag[r + 8]), (diag[r + 8], far[r])]
    return [whole(x, busy) for x in (a, b, c, d)]


def exchange(buffers):
    out = [None] * 4
    for k in ORDER:
        out[k] = lax.ppermute(buffers[k], ("row", "col"), ROUTES[k])
    return out


ROUTES = routes()
ORDER = (1, 0, 2, 3)
ANY = pl.BlockSpec(memory_space=pl.ANY)
VM = pl.BlockSpec(memory_space=pltpu.VMEM)
MIB = 1 << 20


def wide(n):
    return jax.ShapeDtypeStruct((n, BS, BS), F32)


def half(n):
    return jax.ShapeDtypeStruct((n, BS, BS), BF16)


SENT = [half(5), half(5), half(4), half(4)]


def call(kernel, name, out_shape, in_specs, out_specs, scratch, aliases=None, cost=None):
    return pl.pallas_call(
        kernel,
        out_shape=out_shape,
        in_specs=in_specs,
        out_specs=out_specs,
        scratch_shapes=scratch,
        input_output_aliases=aliases or {},
        compiler_params=pltpu.CompilerParams(vmem_limit_bytes=20 * MIB),
        cost_estimate=cost and pl.CostEstimate(flops=cost[0], bytes_accessed=cost[1], transcendentals=0),
        name=name,
    )


def on_device(matrix, factors, inverse, pattern, dropped):
    matrix, factors, inverse, pattern, dropped = (
        pltpu.with_memory_space_constraint(x, pltpu.HBM)
        for x in (matrix, factors, inverse, pattern, dropped)
    )
    table = pltpu.SMEM(pattern.shape, jnp.int32)
    sem = pltpu.SemaphoreType.DMA
    whole_out = jax.ShapeDtypeStruct(factors.shape, F32)

    *sent, held = call(
        cut_kernel, "cut", [*SENT, wide(HELD)], [ANY] * 2, [VM] * 5, [table, sem, sem],
    )(pattern, factors)
    got = exchange(sent)
    out, base, base2, upper_b, a_low, left1, inv, keep = call(
        stage_kernel,
        "stage",
        [whole_out, wide(4), wide(4), half(5), half(8), wide(3), half(inverse.shape[0]),
         jax.ShapeDtypeStruct((8, 8, BS), F32)],
        [ANY] * 5 + [VM],
        [ANY] + [VM] * 7,
        [pltpu.VMEM((64, factors.shape[1]), F32), pltpu.VMEM((6, BS, BS), F32),
         pltpu.VMEM((15, BS, BS), BF16), pltpu.VMEM((8, BS, BS), F32), table, table, sem((4,))],
        cost=(60_000_000, 6_000_000),
    )(pattern, dropped, factors, matrix, inverse, held)
    *sent, diag1, low1 = call(
        middle_kernel, "middle", [*SENT, wide(4), wide(5)], [VM] * 9, [VM] * 6, [],
    )(held, base, upper_b, a_low, inv, *got)
    got2 = exchange(sent)
    out, low1_d = call(
        between_kernel,
        "between",
        [whole_out, wide(5)],
        [VM] * 7 + [ANY],
        [ANY, VM],
        [pltpu.VMEM((3, BS, BS), F32), sem],
        aliases={7: 0},
        cost=(60_000_000, 2_000_000),
    )(held, diag1, left1, a_low, inv, keep, got[1], out)
    return call(
        last_kernel,
        "last",
        whole_out,
        [VM] * 11 + [ANY],
        ANY,
        [pltpu.VMEM((HELD, BS, BS), F32), sem],
        aliases={11: 0},
    )(diag1, base2, low1, low1_d, a_low, inv, keep, *got2, out)


def solution(mesh):
    placed = (
        P("row", "col"),
        P("row", "col"),
        P("col", None, None),
        P("row", "col"),
        P("row", "col"),
    )
    return jax.shard_map(
        on_device, mesh=mesh, in_specs=placed, out_specs=P("row", "col"), check_vma=False
    )
```

profile of v0, /device:TPU:16, one launch (start us, length us, event | category | flops | bytes accessed | tf_op | source)
XLA Modules:
  0.0 25.0 jit_solution(13855408513174904314)
XLA Ops:
  0.0 1.0 %cut.1 = (bf16[5,128,128]{2,1,0:T(8,128)(2,1)S(1)}, bf16[5,128,128]{2,1,0:T(8,128)(2,1)S(1)}, bf16[4,128,128]{2,1,0:T(8,128)(2,1)S(1)}, bf16[4,128,128]{2,1,0:T(8,128)(2,1)S(1)}, f32[9,128,128]{2,1,0:T(8,128)S(1)}) custom-call(s32[4,8]{1,0:T(4,128)} %pattern.3, f32[512,1024]{1,0:T(8,128)} %factors.3), custom_call_target="tpu_custom_call" | custom-call | tf_op jit(solution)/shard_map/cut/pallas_call | solution.py:537
  1.0 0.1 collective-permute-start
  1.1 0.5 %collective-permute-start.1 = (bf16[5,128,128]{2,1,0:T(8,128)(2,1)S(1)}, bf16[5,128,128]{2,1,0:T(8,128)(2,1)S(1)}, u32[]{:S(2)}, u32[]{:S(2)}) collective-permute-start(bf16[5,128,128]{2,1,0:T(8,128)(2,1)S(1)} %get-tuple-element.32), channel_id=1, source_target_pairs={{0,8},{17,25},{34,42},{51,59},{68,76},{85,93},{102,110},{119,127},... | collective-permute-start | bytes 491528 | tf_op jit(solution)/shard_map/ppermute | solution.py:492
  1.6 3.0 %collective-permute-start.2 = (bf16[4,128,128]{2,1,0:T(8,128)(2,1)S(1)}, bf16[4,128,128]{2,1,0:T(8,128)(2,1)S(1)}, u32[]{:S(2)}, u32[]{:S(2)}) collective-permute-start(bf16[4,128,128]{2,1,0:T(8,128)(2,1)S(1)} %get-tuple-element.33), channel_id=1, source_target_pairs={{0,64},{64,68},{68,4},{4,0},{8,72},{72,76},{76,12},{12,8},{17,81},... | collective-permute-start | bytes 393224 | tf_op jit(solution)/shard_map/ppermute | solution.py:492
  4.6 3.5 %collective-permute-start.3 = (bf16[4,128,128]{2,1,0:T(8,128)(2,1)S(1)}, bf16[4,128,128]{2,1,0:T(8,128)(2,1)S(1)}, u32[]{:S(2)}, u32[]{:S(2)}) collective-permute-start(bf16[4,128,128]{2,1,0:T(8,128)(2,1)S(1)} %get-tuple-element.34), channel_id=1, source_target_pairs={{4,68},{68,4},{12,76},{76,12},{21,85},{85,21},{29,93},{93,29},{38,... | collective-permute-start | bytes 393224 | tf_op jit(solution)/shard_map/ppermute | solution.py:492
  8.1 2.2 %stage.1 = (f32[512,1024]{1,0:T(8,128)}, f32[4,128,128]{2,1,0:T(8,128)S(1)}, f32[4,128,128]{2,1,0:T(8,128)S(1)}, bf16[5,128,128]{2,1,0:T(8,128)(2,1)S(1)}, bf16[...) custom-call(s32[4,8]{1,0:T(4,128)} %pattern.3, ...), custom_call_target="tpu_custom_call" | custom-call | flops 60000000 | bytes 6000000 | tf_op jit(solution)/shard_map/stage/pallas_call | solution.py:541
  10.3 2.1 %collective-permute-done.2.rc = bf16[4,128,128]{2,1,0:T(8,128)(2,1)S(1)} collective-permute-done((bf16[4,128,128]{2,1,0:T(8,128)(2,1)S(1)}, bf16[4,128,128]{2,1,0:T(8,128)(2,1)S(1)}, u32[]{:S(2)}, u32[]{:S(2)}) %collective-permute-start.2) | collective-permute-done | bytes 131104 | tf_op jit(solution)/shard_map/ppermute | solution.py:492
  12.4 2.2 %collective-permute-done.3.rd = bf16[4,128,128]{2,1,0:T(8,128)(2,1)S(1)} collective-permute-done((bf16[4,128,128]{2,1,0:T(8,128)(2,1)S(1)}, bf16[4,128,128]{2,1,0:T(8,128)(2,1)S(1)}, u32[]{:S(2)}, u32[]{:S(2)}) %collective-permute-start.3) | collective-permute-done | bytes 131104 | tf_op jit(solution)/shard_map/ppermute | solution.py:492
  14.6 0.0 collective-permute-done.ra
  14.6 0.0 collective-permute-done.1.rb
  14.6 0.1 collective-permute-start.4
  14.7 0.5 %collective-permute-start.5 = (bf16[5,128,128]{2,1,0:T(8,128)(2,1)S(1)}, bf16[5,128,128]{2,1,0:T(8,128)(2,1)S(1)}, u32[]{:S(2)}, u32[]{:S(2)}) collective-permute-start(bf16[5,128,128]{2,1,0:T(8,128)(2,1)S(1)} %get-tuple-element.43), channel_id=1, source_target_pairs={{0,8},{17,25},{34,42},{51,59},{68,76},{85,93},{102,110},{119,127},... | collective-permute-start | bytes 491528 | tf_op jit(solution)/shard_map/ppermute | solution.py:492
  15.2 0.0 collective-permute-start.6
  15.2 3.5 %collective-permute-start.7 = (bf16[4,128,128]{2,1,0:T(8,128)(2,1)S(1)}, bf16[4,128,128]{2,1,0:T(8,128)(2,1)S(1)}, u32[]{:S(2)}, u32[]{:S(2)}) collective-permute-start(bf16[4,128,128]{2,1,0:T(8,128)(2,1)S(1)} %get-tuple-element.45), channel_id=1, source_target_pairs={{4,68},{68,4},{12,76},{76,12},{21,85},{85,21},{29,93},{93,29},{38,... | collective-permute-start | bytes 393224 | tf_op jit(solution)/shard_map/ppermute | solution.py:492
  18.8 4.3 %collective-permute-done.6.rc = bf16[4,128,128]{2,1,0:T(8,128)(2,1)S(1)} collective-permute-done((bf16[4,128,128]{2,1,0:T(8,128)(2,1)S(1)}, bf16[4,128,128]{2,1,0:T(8,128)(2,1)S(1)}, u32[]{:S(2)}, u32[]{:S(2)}) %collective-permute-start.6) | collective-permute-done | bytes 131104 | tf_op jit(solution)/shard_map/ppermute | solution.py:492
  23.1 1.9 %collective-permute-done.7.rd = bf16[4,128,128]{2,1,0:T(8,128)(2,1)S(1)} collective-permute-done((bf16[4,128,128]{2,1,0:T(8,128)(2,1)S(1)}, bf16[4,128,128]{2,1,0:T(8,128)(2,1)S(1)}, u32[]{:S(2)}, u32[]{:S(2)}) %collective-permute-start.7) | collective-permute-done | bytes 131104 | tf_op jit(solution)/shard_map/ppermute | solution.py:492
  25.0 0.0 collective-permute-done.4.ra
  25.0 0.0 collective-permute-done.5.rb
  (3 shorter events, 0.0 us)
Async XLA Ops:
  1.0 13.6 %collective-permute-start = (bf16[5,128,128]{2,1,0:T(8,128)(2,1)S(1)}, bf16[5,128,128]{2,1,0:T(8,128)(2,1)S(1)}, u32[]{:S(2)}, u32[]{:S(2)}) collective-permute-start(bf16[5,128,128]{2,1,0:T(8,128)(2,1)S(1)} %get-tuple-element.31), channel_id=1, source_target_pairs={{0,8},{17,25},{34,42},{51,59},{68,76},{85,93},{102,110},{119,127},... | collective-permute-start | bytes 491528 | tf_op jit(solution)/shard_map/ppermute | solution.py:492
  1.1 13.5 %collective-permute-start.1 = (bf16[5,128,128]{2,1,0:T(8,128)(2,1)S(1)}, bf16[5,128,128]{2,1,0:T(8,128)(2,1)S(1)}, u32[]{:S(2)}, u32[]{:S(2)}) collective-permute-start(bf16[5,128,128]{2,1,0:T(8,128)(2,1)S(1)} %get-tuple-element.32), channel_id=1, source_target_pairs={{0,8},{17,25},{34,42},{51,59},{68,76},{85,93},{102,110},{119,127},... | collective-permute-start | bytes 491528 | tf_op jit(solution)/shard_map/ppermute | solution.py:492
  1.6 10.8 %collective-permute-start.2 = (bf16[4,128,128]{2,1,0:T(8,128)(2,1)S(1)}, bf16[4,128,128]{2,1,0:T(8,128)(2,1)S(1)}, u32[]{:S(2)}, u32[]{:S(2)}) collective-permute-start(bf16[4,128,128]{2,1,0:T(8,128)(2,1)S(1)} %get-tuple-element.33), channel_id=1, source_target_pairs={{0,64},{64,68},{68,4},{4,0},{8,72},{72,76},{76,12},{12,8},{17,81},... | collective-permute-start | bytes 393224 | tf_op jit(solution)/shard_map/ppermute | solution.py:492
  4.6 10.0 %collective-permute-start.3 = (bf16[4,128,128]{2,1,0:T(8,128)(2,1)S(1)}, bf16[4,128,128]{2,1,0:T(8,128)(2,1)S(1)}, u32[]{:S(2)}, u32[]{:S(2)}) collective-permute-start(bf16[4,128,128]{2,1,0:T(8,128)(2,1)S(1)} %get-tuple-element.34), channel_id=1, source_target_pairs={{4,68},{68,4},{12,76},{76,12},{21,85},{85,21},{29,93},{93,29},{38,... | collective-permute-start | bytes 393224 | tf_op jit(solution)/shard_map/ppermute | solution.py:492
  14.6 10.4 %collective-permute-start.4 = (bf16[5,128,128]{2,1,0:T(8,128)(2,1)S(1)}, bf16[5,128,128]{2,1,0:T(8,128)(2,1)S(1)}, u32[]{:S(2)}, u32[]{:S(2)}) collective-permute-start(bf16[5,128,128]{2,1,0:T(8,128)(2,1)S(1)} %get-tuple-element.42), channel_id=1, source_target_pairs={{0,8},{17,25},{34,42},{51,59},{68,76},{85,93},{102,110},{119,127},... | collective-permute-start | bytes 491528 | tf_op jit(solution)/shard_map/ppermute | solution.py:492
  14.7 10.3 %collective-permute-start.5 = (bf16[5,128,128]{2,1,0:T(8,128)(2,1)S(1)}, bf16[5,128,128]{2,1,0:T(8,128)(2,1)S(1)}, u32[]{:S(2)}, u32[]{:S(2)}) collective-permute-start(bf16[5,128,128]{2,1,0:T(8,128)(2,1)S(1)} %get-tuple-element.43), channel_id=1, source_target_pairs={{0,8},{17,25},{34,42},{51,59},{68,76},{85,93},{102,110},{119,127},... | collective-permute-start | bytes 491528 | tf_op jit(solution)/shard_map/ppermute | solution.py:492
  15.2 7.9 %collective-permute-start.6 = (bf16[4,128,128]{2,1,0:T(8,128)(2,1)S(1)}, bf16[4,128,128]{2,1,0:T(8,128)(2,1)S(1)}, u32[]{:S(2)}, u32[]{:S(2)}) collective-permute-start(bf16[4,128,128]{2,1,0:T(8,128)(2,1)S(1)} %get-tuple-element.44), channel_id=1, source_target_pairs={{0,64},{64,68},{68,4},{4,0},{8,72},{72,76},{76,12},{12,8},{17,81},... | collective-permute-start | bytes 393224 | tf_op jit(solution)/shard_map/ppermute | solution.py:492
  15.2 9.8 %collective-permute-start.7 = (bf16[4,128,128]{2,1,0:T(8,128)(2,1)S(1)}, bf16[4,128,128]{2,1,0:T(8,128)(2,1)S(1)}, u32[]{:S(2)}, u32[]{:S(2)}) collective-permute-start(bf16[4,128,128]{2,1,0:T(8,128)(2,1)S(1)} %get-tuple-element.45), channel_id=1, source_target_pairs={{4,68},{68,4},{12,76},{76,12},{21,85},{85,21},{29,93},{93,29},{38,... | collective-permute-start | bytes 393224 | tf_op jit(solution)/shard_map/ppermute | solution.py:492
where the time goes:
time: 25.2 us; the launch traced here: 25 us
  starting transfers between devices  11.2 us (44%)
  waiting for transfers between devices  10.5 us (42%)
  Pallas kernels  3.24 us (13%)
    ppermute x8, starting transfers between devices, exchange(): out[k] = lax.ppermute(buffers[k], ('row', 'col'), ROUTES[k])  11.2 us
    ppermute x8, waiting for transfers between devices, exchange(): out[k] = lax.ppermute(buffers[k], ('row', 'col'), ROUTES[k])  10.5 us
    pallas_call x1, Pallas kernels, on_device(): call(stage_kernel, 'stage', [whole_out, wide(4), wide(4), half(5), half(8...  2.19 us
    pallas_call x1, Pallas kernels, on_device(): call(cut_kernel, 'cut', [*SENT, wide(HELD)], [ANY] * 2, [VM] * 5, [table,...  1 us
  transfers between devices with their start and end apart: 8, of which 4 were waited for; matrix products, arithmetic and copies ran while one was open for 0% of the time, Pallas kernels for 9%

commit v1 on v0

--- a/solution.py
+++ b/solution.py
@@ -102,8 +102,9 @@
     return (table[place] == 1).astype(F32)
 
 
-def cut_kernel(pattern, factors, sa, sb, sc, sd, held, table, sem, table_sem):
+def cut_kernel(plan, pattern, factors, sa, sb, sc, sd, held, table, sem, table_sem):
     w = role()
+    s_near, s_low, s_up = plan.sends(sa, sb, sc, sd)
 
     @pl.when(w["any"])
     def _():
@@ -134,17 +135,17 @@
 
                 @pl.when(w["d_odd"])
                 def _():
-                    sa[j] = value
+                    s_near[j] = value
 
         @pl.when(w["f_early"])
         def _():
             for j in range(4):
-                sd[j] = masked(OFF + j)
+                s_up[j] = masked(OFF + j)
 
         @pl.when(w["f_late"])
         def _():
             for j in range(4):
-                sc[j] = masked(OFF + j)
+                s_low[j] = masked(OFF + j)
 
         @pl.when(w["d_even"] | w["n_odd"])
         def _():
@@ -166,7 +167,7 @@
 
 
 def stage_kernel(pattern, dropped, factors, matrix, inverse, held,
-                 out, base, base2, upper_b, a_low, left1, inv, keep,
+                 out, base, base2, upper_b, upper_f, a_low, left1, inv, keep,
                  zeros, f, a, done, table, drops, sems):
     w = role()
     zeros[...] = jnp.zeros_like(zeros)
@@ -218,7 +219,10 @@
 
                 def act(s=s):
                     one, two = upper(held[s], a[s], spot(w, s))
-                    upper_b[s - X] = one.astype(BF16)
+                    one = one.astype(BF16)
+                    upper_b[s - OFF if s > X else 4] = one
+                    if s > X:
+                        upper_f[s - OFF] = one
                     done[s - X] = two
 
                 act() if s > X else pl.when(w["near_upper"])(act)
@@ -302,40 +306,22 @@
                     emit(j, at(j, near, far))
 
 
-def middle_kernel(held, base, upper_b, a_low, inv, ra, rb, rc, rd,
-                  sa, sb, sc, sd, diag1, low1):
+def middle_kernel(plan, held, base, a_low, inv, ra, rb, rc, rd, sb, sc, diag1, low1):
     w = role()
+    r_near, r_low, r_up = plan.sends(ra, rb, rc, rd)
 
     def emit(j, total):
         old = held[DIAG + j]
         one = old + (total - old)
         diag1[j] = one
         value = one.astype(BF16)
-
-        @pl.when(w["even"])
-        def _():
-            sb[j] = value
-
-        @pl.when(w["d_odd"])
-        def _():
-            sa[j] = value
+        sb[j] = value
 
         @pl.when(w["d_early"])
         def _():
             sc[j] = value
 
-    each_diagonal(w, emit, base, held, rb, ra, rc, rd)
-
-    @pl.when(w["d_even"] | w["n_odd"])
-    def _():
-        for j in range(4):
-            sa[j] = upper_b[1 + j]
-        sa[4] = upper_b[0]
-
-    @pl.when(w["f_early"])
-    def _():
-        for j in range(4):
-            sd[j] = upper_b[1 + j]
+    each_diagonal(w, emit, base, held, rb, ra, r_low, r_up)
 
     def lower(dst, u, j, s):
         one = lower_step(held[s], a_low[s - X], u[j], inv[w["off"] + j])
@@ -345,8 +331,8 @@
     @pl.when(w["n_even"])
     def _():
         for j in range(4):
-            lower(sb, ra, j, OFF + j)
-        lower(sb, ra, 3, X)
+            lower(sb, r_near, j, OFF + j)
+        lower(sb, r_near, 3, X)
 
     @pl.when(w["f_late"])
     def _():
@@ -377,10 +363,11 @@
         writes.run(False)
 
 
-def last_kernel(diag1, base2, low1, low1_d, a_low, inv, keep, ra, rb, rc, rd, out_in,
+def last_kernel(plan, diag1, base2, low1, low1_d, a_low, inv, keep, ra, rb, rc, rd, out_in,
                 out, done, sem):
     del out_in
     w = role()
+    r_near, r_low, r_up = plan.sends(ra, rb, rc, rd)
     writes = Copies(sem)
     for j in range(4):
         writes.add(w["d"], done.at[j], block(out, *spot(w, j)))
@@ -396,13 +383,13 @@
         old = diag1[j]
         done[DIAG + j] = old + (total - old)
 
-    each_diagonal(w, emit, base2, Own(), rb, ra, rc, rd)
+    each_diagonal(w, emit, base2, Own(), rb, ra, r_low, r_up)
 
     def lower(old, u, j, s):
         two = lower_step(old[s - X], a_low[s - X], u[j], inv[w["off"] + j])
         done[s] = two * keep[s - X, 0:1, :]
 
-    for name, old, u in (("d_odd", low1_d, rb), ("n_even", low1, ra), ("f_late", low1, rc)):
+    for name, old, u in (("d_odd", low1_d, rb), ("n_even", low1, r_near), ("f_late", low1, rc)):
 
         @pl.when(w[name])
         def _():
@@ -466,35 +453,45 @@
     return list(pairs) + [(a, free_b[pick[i]]) for i, a in enumerate(free_a)]
 
 
-def routes():
-    def at(r, c):
-        return r * 8 + c
-
-    diag = [at(r, r // 2) for r in range(16)]
-    near = {r: at(r, r // 2 + (1 if r % 2 else -1)) for r in range(1, 15)}
-    far = [at(r, r // 2 + (4 if r < 8 else -4)) for r in range(16)]
-    busy = {*diag, *near.values(), *far}
-    pair = [(diag[r], diag[r + 1]) for r in range(0, 16, 2)]
-    a = pair + [(diag[r], near[r + 1]) for r in range(1, 14, 2)]
-    a += [(near[r], diag[r + 1]) for r in range(1, 14, 2)]
-    b = pair + [(near[r], diag[r]) for r in range(2, 15, 2)]
-    c, d = [], []
-    for r in range(8):
-        ring = [diag[r], far[r + 8], diag[r + 8], far[r]]
-        c += list(zip(ring, ring[1:] + ring[:1]))
-        d += [(far[r], diag[r + 8]), (diag[r + 8], far[r])]
-    return [whole(x, busy) for x in (a, b, c, d)]
-
-
-def exchange(buffers):
+class Plan:
+    def __init__(self, near, far_low, order, routes=None):
+        self.near, self.far_low, self.order = near, far_low, order
+        self.routes = routes
+
+    def sends(self, *bufs):
+        return bufs[self.near], bufs[self.far_low], bufs[5 - self.far_low]
+
+    def needed(self):
+        def at(r, c):
+            return r * 8 + c
+
+        diag = [at(r, r // 2) for r in range(16)]
+        near = {r: at(r, r // 2 + (1 if r % 2 else -1)) for r in range(1, 15)}
+        far = [at(r, r // 2 + (4 if r < 8 else -4)) for r in range(16)]
+        pair = [(diag[r], diag[r + 1]) for r in range(0, 16, 2)]
+        out = [list(pair), list(pair), [], []]
+        out[0] += [(near[r], diag[r + 1]) for r in range(1, 14, 2)]
+        out[1] += [(near[r], diag[r]) for r in range(2, 15, 2)]
+        out[self.near] += [(diag[r], near[r + 1]) for r in range(1, 14, 2)]
+        out[2] += [(diag[r], far[r + 8]) for r in range(8)]
+        out[self.far_low] += [(far[r], diag[r]) for r in range(8, 16)]
+        out[5 - self.far_low] += [(far[r], diag[r + 8]) for r in range(8)]
+        return out, {*diag, *near.values(), *far}
+
+    def full(self):
+        needed, busy = self.needed()
+        return self.routes or [whole(x, busy) for x in needed]
+
+
+def exchange(plan, buffers):
     out = [None] * 4
-    for k in ORDER:
-        out[k] = lax.ppermute(buffers[k], ("row", "col"), ROUTES[k])
+    routes = plan.full()
+    for k in plan.order:
+        out[k] = lax.ppermute(buffers[k], ("row", "col"), routes[k])
     return out
 
 
-ROUTES = routes()
-ORDER = (1, 0, 2, 3)
+PLANS = [Plan(0, 2, (1, 0, 2, 3)), Plan(1, 2, (0, 3, 1, 2))]
 ANY = pl.BlockSpec(memory_space=pl.ANY)
 VM = pl.BlockSpec(memory_space=pltpu.VMEM)
 MIB = 1 << 20
@@ -508,7 +505,11 @@
     return jax.ShapeDtypeStruct((n, BS, BS), BF16)
 
 
-SENT = [half(5), half(5), half(4), half(4)]
+def sent_shapes(plan):
+    rows = [None] * 4
+    for place, k in enumerate(plan.order):
+        rows[k] = 5 if any(j < 2 for j in plan.order[place:]) else 4
+    return [half(n) for n in rows]
 
 
 def call(kernel, name, out_shape, in_specs, out_specs, scratch, aliases=None, cost=None):
@@ -534,25 +535,28 @@
     sem = pltpu.SemaphoreType.DMA
     whole_out = jax.ShapeDtypeStruct(factors.shape, F32)
 
+    plan, next_plan = PLANS
     *sent, held = call(
-        cut_kernel, "cut", [*SENT, wide(HELD)], [ANY] * 2, [VM] * 5, [table, sem, sem],
+        functools.partial(cut_kernel, plan), "cut", [*sent_shapes(plan), wide(HELD)],
+        [ANY] * 2, [VM] * 5, [table, sem, sem],
     )(pattern, factors)
-    got = exchange(sent)
-    out, base, base2, upper_b, a_low, left1, inv, keep = call(
+    got = exchange(plan, sent)
+    out, base, base2, upper_b, upper_f, a_low, left1, inv, keep = call(
         stage_kernel,
         "stage",
-        [whole_out, wide(4), wide(4), half(5), half(8), wide(3), half(inverse.shape[0]),
+        [whole_out, wide(4), wide(4), half(5), half(5), half(8), wide(3), half(inverse.shape[0]),
          jax.ShapeDtypeStruct((8, 8, BS), F32)],
         [ANY] * 5 + [VM],
-        [ANY] + [VM] * 7,
+        [ANY] + [VM] * 8,
         [pltpu.VMEM((64, factors.shape[1]), F32), pltpu.VMEM((6, BS, BS), F32),
          pltpu.VMEM((15, BS, BS), BF16), pltpu.VMEM((8, BS, BS), F32), table, table, sem((4,))],
         cost=(60_000_000, 6_000_000),
     )(pattern, dropped, factors, matrix, inverse, held)
-    *sent, diag1, low1 = call(
-        middle_kernel, "middle", [*SENT, wide(4), wide(5)], [VM] * 9, [VM] * 6, [],
-    )(held, base, upper_b, a_low, inv, *got)
-    got2 = exchange(sent)
+    sent_b, sent_c, diag1, low1 = call(
+        functools.partial(middle_kernel, plan), "middle",
+        [half(5), half(4), wide(4), wide(5)], [VM] * 8, [VM] * 4, [],
+    )(held, base, a_low, inv, *got)
+    got2 = exchange(next_plan, (upper_b, sent_b, sent_c, upper_f))
     out, low1_d = call(
         between_kernel,
         "between",
@@ -564,7 +568,7 @@
         cost=(60_000_000, 2_000_000),
     )(held, diag1, left1, a_low, inv, keep, got[1], out)
     return call(
-        last_kernel,
+        functools.partial(last_kernel, next_plan),
         "last",
         whole_out,
         [VM] * 11 + [ANY],

time: 25.2 us -> 21.8 us (0.87)
  the two profiles are of different devices: /device:TPU:16 before, /device:TPU:1 now
where the time goes in v1:
time: 21.8 us; the launch traced here: 21.5 us
  starting transfers between devices  9.08 us (42%)
  Pallas kernels  7.77 us (36%)
  waiting for transfers between devices  4.63 us (21%)
    ppermute x8, starting transfers between devices, exchange(): out[k] = lax.ppermute(buffers[k], ('row', 'col'), routes[k])  9.08 us
    ppermute x8, waiting for transfers between devices, exchange(): out[k] = lax.ppermute(buffers[k], ('row', 'col'), routes[k])  4.63 us
    pallas_call x1, Pallas kernels, on_device(): call(stage_kernel, 'stage', [whole_out, wide(4), wide(4), half(5), half(5...  3.54 us
    pallas_call x1, Pallas kernels, on_device(): call(functools.partial(last_kernel, next_plan), 'last', whole_out, [VM] *...  1.35 us
    pallas_call x1, Pallas kernels, on_device(): call(functools.partial(cut_kernel, plan), 'cut', [*sent_shapes(plan), wid...  1.24 us
    pallas_call x1, Pallas kernels, on_device(): call(between_kernel, 'between', [whole_out, wide(5)], [VM] * 7 + [ANY], [...  0.98 us
    pallas_call x1, Pallas kernels, on_device(): call(functools.partial(middle_kernel, plan), 'middle', [half(5), half(4),...  0.66 us
  transfers between devices with their start and end apart: 8, of which 2 were waited for; matrix products, arithmetic and copies ran while one was open for 0% of the time, Pallas kernels for 24%

profile of v1, /device:TPU:1, one launch (start us, length us, event | category | flops | bytes accessed | tf_op | source)
XLA Modules:
  0.0 21.5 jit_solution(2969450625715880256)
XLA Ops:
  0.0 1.2 %cut.1 = (bf16[5,128,128]{2,1,0:T(8,128)(2,1)S(1)}, bf16[5,128,128]{2,1,0:T(8,128)(2,1)S(1)}, bf16[4,128,128]{2,1,0:T(8,128)(2,1)S(1)}, bf16[4,128,128]{2,1,0:T(8,128)(2,1)S(1)}, f32[9,128,128]{2,1,0:T(8,128)S(1)}) custom-call(s32[4,8]{1,0:T(4,128)} %pattern.3, f32[512,1024]{1,0:T(8,128)} %factors.3), custom_call_target="tpu_custom_call" | custom-call | tf_op jit(solution)/shard_map/cut/pallas_call | solution.py:539
  1.3 4.0 %collective-permute-start = (bf16[5,128,128]{2,1,0:T(8,128)(2,1)S(1)}, bf16[5,128,128]{2,1,0:T(8,128)(2,1)S(1)}, u32[]{:S(2)}, u32[]{:S(2)}) collective-permute-start(bf16[5,128,128]{2,1,0:T(8,128)(2,1)S(1)} %get-tuple-element.29), channel_id=1, source_target_pairs={{0,8},{17,25},{34,42},{51,59},{68,76},{85,93},{102,110},{119,127},... | collective-permute-start | bytes 491528 | tf_op jit(solution)/shard_map/ppermute | solution.py:490
  5.2 0.0 collective-permute-start.1
  5.2 1.0 %collective-permute-start.2 = (bf16[4,128,128]{2,1,0:T(8,128)(2,1)S(1)}, bf16[4,128,128]{2,1,0:T(8,128)(2,1)S(1)}, u32[]{:S(2)}, u32[]{:S(2)}) collective-permute-start(bf16[4,128,128]{2,1,0:T(8,128)(2,1)S(1)} %get-tuple-element.31), channel_id=1, source_target_pairs={{0,64},{8,72},{17,81},{25,89},{34,98},{42,106},{51,115},{59,123},{... | collective-permute-start | bytes 393224 | tf_op jit(solution)/shard_map/ppermute | solution.py:490
  6.3 0.7 %collective-permute-start.3 = (bf16[4,128,128]{2,1,0:T(8,128)(2,1)S(1)}, bf16[4,128,128]{2,1,0:T(8,128)(2,1)S(1)}, u32[]{:S(2)}, u32[]{:S(2)}) collective-permute-start(bf16[4,128,128]{2,1,0:T(8,128)(2,1)S(1)} %get-tuple-element.32), channel_id=1, source_target_pairs={{4,68},{12,76},{21,85},{29,93},{38,102},{46,110},{55,119},{63,127}... | collective-permute-start | bytes 393224 | tf_op jit(solution)/shard_map/ppermute | solution.py:490
  7.0 3.5 %stage.1 = (f32[512,1024]{1,0:T(8,128)}, f32[4,128,128]{2,1,0:T(8,128)S(1)}, f32[4,128,128]{2,1,0:T(8,128)S(1)}, bf16[5,128,128]{2,1,0:T(8,128)(2,1)S(1)}, bf16[...) custom-call(s32[4,8]{1,0:T(4,128)} %pattern.3, ...), custom_call_target="tpu_custom_call" | custom-call | flops 60000000 | bytes 6000000 | tf_op jit(solution)/shard_map/stage/pallas_call | solution.py:544
  10.5 0.2 %collective-permute-start.4 = (bf16[5,128,128]{2,1,0:T(8,128)(2,1)S(1)}, bf16[5,128,128]{2,1,0:T(8,128)(2,1)S(1)}, u32[]{:S(2)}, u32[]{:S(2)}) collective-permute-start(bf16[5,128,128]{2,1,0:T(8,128)(2,1)S(1)} %get-tuple-element.40), channel_id=1, source_target_pairs={{0,8},{17,25},{34,42},{51,59},{68,76},{85,93},{102,110},{119,127},... | collective-permute-start | bytes 491528 | tf_op jit(solution)/shard_map/ppermute | solution.py:490
  10.7 1.4 %collective-permute-done.2.rc = bf16[4,128,128]{2,1,0:T(8,128)(2,1)S(1)} collective-permute-done((bf16[4,128,128]{2,1,0:T(8,128)(2,1)S(1)}, bf16[4,128,128]{2,1,0:T(8,128)(2,1)S(1)}, u32[]{:S(2)}, u32[]{:S(2)}) %collective-permute-start.2) | collective-permute-done | bytes 131104 | tf_op jit(solution)/shard_map/ppermute | solution.py:490
  12.2 0.4 %collective-permute-start.7 = (bf16[5,128,128]{2,1,0:T(8,128)(2,1)S(1)}, bf16[5,128,128]{2,1,0:T(8,128)(2,1)S(1)}, u32[]{:S(2)}, u32[]{:S(2)}) collective-permute-start(bf16[5,128,128]{2,1,0:T(8,128)(2,1)S(1)} %get-tuple-element.43), channel_id=1, source_target_pairs={{4,68},{12,76},{21,85},{29,93},{38,102},{46,110},{55,119},{63,127}... | collective-permute-start | bytes 491528 | tf_op jit(solution)/shard_map/ppermute | solution.py:490
  12.6 0.0 collective-permute-done.3.rd
  12.6 0.0 collective-permute-done.ra
  12.6 0.0 collective-permute-done.1.rb
  12.6 0.7 %middle.1 = (bf16[5,128,128]{2,1,0:T(8,128)(2,1)S(1)}, bf16[4,128,128]{2,1,0:T(8,128)(2,1)S(1)}, f32[4,128,128]{2,1,0:T(8,128)S(1)}, f32[5,128,128]{2,1,0:T(8,128)S(1)}) custom-call(f32[9,128,128]{2,1,0:T(8,128)S(1)} %get-tuple-element.25.held, f32[4,128,128]{2,1,0:T(8,128)S(1)} %get-tuple-element.26.base, bf16[8,128,128]{2,1,0:T(8,128)(2,1)S(1)} %get-tuple-element.27.a_low, ...), custom_call_target="tpu_custom_call" | custom-call | tf_op jit(solution)/shard_map/middle/pallas_call | solution.py:555
  13.2 0.1 collective-permute-start.5
  13.3 2.6 %collective-permute-start.6 = (bf16[4,128,128]{2,1,0:T(8,128)(2,1)S(1)}, bf16[4,128,128]{2,1,0:T(8,128)(2,1)S(1)}, u32[]{:S(2)}, u32[]{:S(2)}) collective-permute-start(bf16[4,128,128]{2,1,0:T(8,128)(2,1)S(1)} %get-tuple-element.42), channel_id=1, source_target_pairs={{0,64},{8,72},{17,81},{25,89},{34,98},{42,106},{51,115},{59,123},{... | collective-permute-start | bytes 393224 | tf_op jit(solution)/shard_map/ppermute | solution.py:490
  16.0 1.0 %between.1 = (f32[512,1024]{1,0:T(8,128)}, f32[5,128,128]{2,1,0:T(8,128)S(1)}) custom-call(f32[9,128,128]{2,1,0:T(8,128)S(1)} %get-tuple-element.25.held, f32[4,128,128]{2,1,0:T(8,128)S(1)} %get-tuple-element.33.diag1, f32[3,128,128]{2,1,0:T(8,128)S(1)} %get-tuple-element.36.left1, ...), custom_call_target="tpu_custom_call", output_to_operand_aliasing={{0}: (7, {})} | custom-call | flops 60000000 | bytes 2000000 | tf_op jit(solution)/shard_map/between/pallas_call | solution.py:560
  17.0 0.0 collective-permute-done.4.ra
  17.0 0.0 collective-permute-done.7.rd
  17.0 3.2 %collective-permute-done.6.rc = bf16[4,128,128]{2,1,0:T(8,128)(2,1)S(1)} collective-permute-done((bf16[4,128,128]{2,1,0:T(8,128)(2,1)S(1)}, bf16[4,128,128]{2,1,0:T(8,128)(2,1)S(1)}, u32[]{:S(2)}, u32[]{:S(2)}) %collective-permute-start.6) | collective-permute-done | bytes 131104 | tf_op jit(solution)/shard_map/ppermute | solution.py:490
  20.2 0.0 collective-permute-done.5.rb
  20.2 1.3 %last.1 = f32[512,1024]{1,0:T(8,128)} custom-call(f32[4,128,128]{2,1,0:T(8,128)S(1)} %get-tuple-element.33.diag1, f32[4,128,128]{2,1,0:T(8,128)S(1)} %get-tuple-element.34.base2, f32[5,128,128]{2,1,0:T(8,128)S(1)} %get-tuple-element.35.low1, f32[5,128,128]{2,1,0:T(8,128)S(1)} %get-tuple-element.39.low1_d, ...), custom_call_target="tpu_custom_call", output_to_operand_aliasing={{}: (11, {})} | custom-call | tf_op jit(solution)/shard_map/last/pallas_call | solution.py:570
Async XLA Ops:
  1.3 11.3 %collective-permute-start = (bf16[5,128,128]{2,1,0:T(8,128)(2,1)S(1)}, bf16[5,128,128]{2,1,0:T(8,128)(2,1)S(1)}, u32[]{:S(2)}, u32[]{:S(2)}) collective-permute-start(bf16[5,128,128]{2,1,0:T(8,128)(2,1)S(1)} %get-tuple-element.29), channel_id=1, source_target_pairs={{0,8},{17,25},{34,42},{51,59},{68,76},{85,93},{102,110},{119,127},... | collective-permute-start | bytes 491528 | tf_op jit(solution)/shard_map/ppermute | solution.py:490
  5.2 7.3 %collective-permute-start.1 = (bf16[5,128,128]{2,1,0:T(8,128)(2,1)S(1)}, bf16[5,128,128]{2,1,0:T(8,128)(2,1)S(1)}, u32[]{:S(2)}, u32[]{:S(2)}) collective-permute-start(bf16[5,128,128]{2,1,0:T(8,128)(2,1)S(1)} %get-tuple-element.30), channel_id=1, source_target_pairs={{0,8},{17,25},{34,42},{51,59},{68,76},{85,93},{102,110},{119,127},... | collective-permute-start | bytes 491528 | tf_op jit(solution)/shard_map/ppermute | solution.py:490
  5.2 6.9 %collective-permute-start.2 = (bf16[4,128,128]{2,1,0:T(8,128)(2,1)S(1)}, bf16[4,128,128]{2,1,0:T(8,128)(2,1)S(1)}, u32[]{:S(2)}, u32[]{:S(2)}) collective-permute-start(bf16[4,128,128]{2,1,0:T(8,128)(2,1)S(1)} %get-tuple-element.31), channel_id=1, source_target_pairs={{0,64},{8,72},{17,81},{25,89},{34,98},{42,106},{51,115},{59,123},{... | collective-permute-start | bytes 393224 | tf_op jit(solution)/shard_map/ppermute | solution.py:490
  6.3 6.3 %collective-permute-start.3 = (bf16[4,128,128]{2,1,0:T(8,128)(2,1)S(1)}, bf16[4,128,128]{2,1,0:T(8,128)(2,1)S(1)}, u32[]{:S(2)}, u32[]{:S(2)}) collective-permute-start(bf16[4,128,128]{2,1,0:T(8,128)(2,1)S(1)} %get-tuple-element.32), channel_id=1, source_target_pairs={{4,68},{12,76},{21,85},{29,93},{38,102},{46,110},{55,119},{63,127}... | collective-permute-start | bytes 393224 | tf_op jit(solution)/shard_map/ppermute | solution.py:490
  10.5 6.5 %collective-permute-start.4 = (bf16[5,128,128]{2,1,0:T(8,128)(2,1)S(1)}, bf16[5,128,128]{2,1,0:T(8,128)(2,1)S(1)}, u32[]{:S(2)}, u32[]{:S(2)}) collective-permute-start(bf16[5,128,128]{2,1,0:T(8,128)(2,1)S(1)} %get-tuple-element.40), channel_id=1, source_target_pairs={{0,8},{17,25},{34,42},{51,59},{68,76},{85,93},{102,110},{119,127},... | collective-permute-start | bytes 491528 | tf_op jit(solution)/shard_map/ppermute | solution.py:490
  12.2 4.8 %collective-permute-start.7 = (bf16[5,128,128]{2,1,0:T(8,128)(2,1)S(1)}, bf16[5,128,128]{2,1,0:T(8,128)(2,1)S(1)}, u32[]{:S(2)}, u32[]{:S(2)}) collective-permute-start(bf16[5,128,128]{2,1,0:T(8,128)(2,1)S(1)} %get-tuple-element.43), channel_id=1, source_target_pairs={{4,68},{12,76},{21,85},{29,93},{38,102},{46,110},{55,119},{63,127}... | collective-permute-start | bytes 491528 | tf_op jit(solution)/shard_map/ppermute | solution.py:490
  13.2 7.0 %collective-permute-start.5 = (bf16[5,128,128]{2,1,0:T(8,128)(2,1)S(1)}, bf16[5,128,128]{2,1,0:T(8,128)(2,1)S(1)}, u32[]{:S(2)}, u32[]{:S(2)}) collective-permute-start(bf16[5,128,128]{2,1,0:T(8,128)(2,1)S(1)} %get-tuple-element.41), channel_id=1, source_target_pairs={{0,8},{17,25},{34,42},{51,59},{68,76},{85,93},{102,110},{119,127},... | collective-permute-start | bytes 491528 | tf_op jit(solution)/shard_map/ppermute | solution.py:490
  13.3 6.8 %collective-permute-start.6 = (bf16[4,128,128]{2,1,0:T(8,128)(2,1)S(1)}, bf16[4,128,128]{2,1,0:T(8,128)(2,1)S(1)}, u32[]{:S(2)}, u32[]{:S(2)}) collective-permute-start(bf16[4,128,128]{2,1,0:T(8,128)(2,1)S(1)} %get-tuple-element.42), channel_id=1, source_target_pairs={{0,64},{8,72},{17,81},{25,89},{34,98},{42,106},{51,115},{59,123},{... | collective-permute-start | bytes 393224 | tf_op jit(solution)/shard_map/ppermute | solution.py:490

commit v2 on v0

v2 whole, which is shorter than its diff:
```python
import functools

import jax
import jax.numpy as jnp
from jax import lax
from jax.experimental import pallas as pl
from jax.experimental.pallas import tpu as pltpu
from jax.sharding import PartitionSpec as P

BS = 128
F32 = jnp.float32
BF16 = jnp.bfloat16

DIAG, X, OFF = 0, 4, 5
HELD = 9


def role():
    r, c = lax.axis_index("row"), lax.axis_index("col")
    odd = lax.rem(r, 2)
    home = lax.div(r, 2)
    late = r >= 8
    is_odd = odd == 1
    even = odd == 0
    is_d = c == home
    is_n = jnp.where(is_odd, c == home + 1, c == home - 1)
    is_f = jnp.where(late, c == home - 4, c == home + 4)
    lower = (is_d & is_odd) | (is_n & even) | (is_f & late)
    held = is_d | is_n | is_f
    return dict(
        even=even,
        top=r == 0,
        d=is_d,
        d_even=is_d & even,
        d_odd=is_d & is_odd,
        d_late=is_d & late,
        d_early=is_d & jnp.logical_not(late),
        n_even=is_n & even,
        n_odd=is_n & is_odd,
        f=is_f,
        f_late=is_f & late,
        f_early=is_f & jnp.logical_not(late),
        near=is_d | is_n,
        any=held,
        lower=lower,
        near_lower=lower & jnp.logical_not(is_f),
        upper=held & jnp.logical_not(lower),
        near_upper=held & jnp.logical_not(lower) & jnp.logical_not(is_f),
        first=4 * odd,
        off=jnp.where(is_f, 4 * odd, 4 * (1 - odd)),
        x_row=jnp.where(is_odd, jnp.where(is_d, 0, 3), jnp.where(is_d, 3, 0)),
        x_col=jnp.where(is_odd, jnp.where(is_d, 3, 0), jnp.where(is_d, 4, 7)),
    )


def spot(w, slot):
    if slot == X:
        return w["x_row"], w["x_col"]
    if slot < X:
        return slot, w["first"] + slot
    return slot - OFF, w["off"] + slot - OFF


def block(ref, i, c):
    return ref.at[pl.ds(pl.multiple_of(i * BS, BS), BS), pl.ds(pl.multiple_of(c * BS, BS), BS)]


def dot(a, b):
    return jnp.dot(a, b, preferred_element_type=F32)


class Copies:
    def __init__(self, sem):
        self.sem, self.todo = sem, []

    def add(self, when, src, dst):
        self.todo.append((when, src, dst))

    def run(self, start):
        i = 0
        while i < len(self.todo):
            when = self.todo[i][0]
            j = i
            while j < len(self.todo) and self.todo[j][0] is when:
                j += 1
            some = self.todo[i:j]

            def act(some=some):
                for _, src, dst in some:
                    copy = pltpu.make_async_copy(src, dst, self.sem)
                    copy.start() if start else copy.wait()

            if when is None:
                act()
            else:
                pl.when(when)(act)
            i = j


def member(table, place):
    return (table[place] == 1).astype(F32)


def cut_kernel(pattern, factors, sa, sb, sc, sd, held, table, sem, table_sem):
    w = role()

    @pl.when(w["any"])
    def _():
        get_table = pltpu.make_async_copy(pattern, table, table_sem)
        get_table.start()
        blocks = Copies(sem)
        for s in range(HELD):
            when = w["d"] if s < X else w["near"] if s == X else None
            blocks.add(when, block(factors, *spot(w, s)), held.at[s])
        blocks.run(True)
        get_table.wait()
        blocks.run(False)

        def masked(s):
            value = held[s] * member(table, spot(w, s))
            held[s] = value
            return value.astype(BF16)

        @pl.when(w["d"])
        def _():
            for j in range(4):
                value = masked(DIAG + j)
                sc[j] = value

                @pl.when(w["even"])
                def _():
                    sb[j] = value

                @pl.when(w["d_odd"])
                def _():
                    sa[j] = value

        @pl.when(w["f_early"])
        def _():
            for j in range(4):
                sd[j] = masked(OFF + j)

        @pl.when(w["f_late"])
        def _():
            for j in range(4):
                sc[j] = masked(OFF + j)

        @pl.when(w["d_even"] | w["n_odd"])
        def _():
            for j in range(4):
                sa[j] = masked(OFF + j)
            sa[4] = masked(X)

        @pl.when(w["n_even"])
        def _():
            for j in range(4):
                sb[j] = masked(OFF + j)
            sb[4] = masked(X)

        @pl.when(w["d_odd"])
        def _():
            for j in range(4):
                masked(OFF + j)
            masked(X)


def kept(drops, place):
    return (1 - drops[place]).astype(F32)


def upper(table, drops, old, a_block, place):
    m = member(table, place)
    a_block = a_block.astype(F32)
    one = old + (a_block - old) * m
    return one, (one + (a_block - one) * m) * kept(drops, place)


def upper_kernel(pattern, dropped, matrix, held, upper_b, upper_f, done, a, table, drops, sems):
    w = role()

    @pl.when(w["upper"])
    def _():
        loads = Copies(sems.at[0])
        loads.add(None, pattern, table)
        loads.add(None, dropped, drops)
        blocks = Copies(sems.at[1])
        for s in range(OFF, HELD):
            blocks.add(None, block(matrix, *spot(w, s)), a.at[s - X])
        blocks.add(w["near_upper"], block(matrix, *spot(w, X)), a.at[0])
        loads.run(True)
        blocks.run(True)
        loads.run(False)
        blocks.run(False)
        for s in range(X, HELD):

            def act(s=s):
                one, done[s - X] = upper(table, drops, held[s], a[s - X], spot(w, s))
                one = one.astype(BF16)
                upper_b[s - OFF if s > X else 4] = one
                if s > X:
                    upper_f[s - OFF] = one

            act() if s > X else pl.when(w["near_upper"])(act)


def right_of(w):
    return [(j, w["first"] + j + 1) for j in range(3)]


def stage_kernel(pattern, dropped, factors, matrix, inverse, held,
                 base, base2, a_low, left1, inv, keep, done,
                 f, a, table, drops, sems):
    w = role()
    tables = Copies(sems.at[1])
    tables.add(None, pattern, table)
    tables.add(None, dropped, drops)
    blocks = Copies(sems.at[2])
    right = right_of(w)
    left = [(j + 1, w["first"] + j) for j in range(3)]
    for k, place in enumerate(right + left):
        blocks.add(w["d"], block(factors, *place), f.at[k])
    for s in range(X):
        blocks.add(w["d"], block(matrix, *spot(w, s)), a.at[s])
    for k, place in enumerate(right + left):
        blocks.add(w["d"], block(matrix, *place), a.at[HELD + k])
    blocks.add(w["near_lower"], block(matrix, *spot(w, X)), a.at[X])
    for s in range(OFF, HELD):
        blocks.add(w["lower"], block(matrix, *spot(w, s)), a.at[s])
    blocks.add(None, inverse, inv)

    @pl.when(w["any"])
    def _():
        tables.run(True)
        blocks.run(True)
        tables.run(False)
        blocks.run(False)

        @pl.when(w["lower"])
        def _():
            for s in range(X, HELD):

                def act(s=s):
                    place = spot(w, s)
                    a_low[s - X] = (a[s].astype(F32) * member(table, place)).astype(BF16)
                    keep[s - X] = jnp.full(keep.shape[1:], kept(drops, place))

                act() if s > X else pl.when(w["near_lower"])(act)

        @pl.when(w["d"])
        def _():
            base[0] = a[0].astype(F32)
            base2[0] = a[0].astype(F32)
            for j in range(3):
                old_u = f[j] * member(table, right[j])
                one_u, done[j] = upper(table, drops, old_u, a[HELD + j], right[j])
                m = member(table, left[j])
                old = f[3 + j] * m
                old_b = old.astype(BF16)
                a_block = a[HELD + 3 + j].astype(F32) * m
                residual = a_block - dot(old_b, held[DIAG + j].astype(BF16)) * m
                one = old + dot(residual.astype(BF16), inv[w["first"] + j]) * m
                left1[j] = one
                a_low[5 + j] = a_block.astype(BF16)
                keep[5 + j] = jnp.full(keep.shape[1:], kept(drops, left[j]))
                a_diag = a[j + 1].astype(F32)
                base[j + 1] = a_diag - dot(old_b, old_u.astype(BF16))
                base2[j + 1] = a_diag - dot(one.astype(BF16), one_u.astype(BF16))


def diagonal(w, sums, l_near, l_x, ra, rc, rd):
    def at(j, with_near, with_far):
        total = sums[j]
        if with_near:
            total = total - dot(l_near(j), ra[j])
        if with_near and j == 0:
            total = total - dot(l_x(), ra[4])
        if with_far:
            total = total - dot(rc[j], rd[j])
        return total

    return at


def lower_step(old, a_block, u, inv_block):
    residual = a_block.astype(F32) - dot(old.astype(BF16), u)
    return old + dot(residual.astype(BF16), inv_block)


def each_diagonal(w, late, emit, sums, own, rb, ra, rc, rd):
    for parity, l_near, l_x in (
        ("d_even", lambda j: rb[j], lambda: rb[4]),
        ("d_odd", lambda j: own[OFF + j].astype(BF16), lambda: own[X].astype(BF16)),
    ):
        at = diagonal(w, sums, l_near, l_x, ra, rc, rd)
        for near in (True,) if late or parity == "d_odd" else (False, True):
            when = w["d_late"] if late else w["d_early"] & (w["top"] != near)

            @pl.when(w[parity] & when)
            def _():
                for j in range(4):
                    emit(j, at(j, near, late))


def middle_kernel(late, held, base, a_low, inv, *refs):
    w = role()
    if late:
        ra, rb, rc, rd, _, _, _, sb, diag1, low1, s_far = refs
    else:
        (ra, rb, sb, diag1, low1, s_far), rc, rd = refs, None, None

    def emit(j, total):
        old = held[DIAG + j]
        one = old + (total - old)
        diag1[j] = one
        value = one.astype(BF16)
        sb[j] = value
        if not late:
            s_far[j] = value

    each_diagonal(w, late, emit, base, held, rb, ra, rc, rd)

    def lower(dst, u, j, s):
        one = lower_step(held[s], a_low[s - X], u[j], inv[w["off"] + j])
        low1[s - X] = one
        dst[s - OFF if s > X else 4] = one.astype(BF16)

    if late:

        @pl.when(w["f_late"])
        def _():
            for j in range(4):
                lower(s_far, rc, j, OFF + j)

    else:

        @pl.when(w["n_even"])
        def _():
            for j in range(4):
                lower(sb, ra, j, OFF + j)
            lower(sb, ra, 3, X)


def between_kernel(held, diag1, left1, a_low, inv, keep, rb, done_up, done_right, out, low1, zeros, done, sems):
    w = role()
    zeros[...] = jnp.zeros_like(zeros)
    rows = zeros.shape[0]
    fill = Copies(sems.at[0])
    for k in range(out.shape[0] // rows):
        fill.add(None, zeros, out.at[pl.ds(k * rows, rows)])
    fill.run(True)
    writes = Copies(sems.at[1])
    for s in range(OFF, HELD):
        writes.add(w["upper"], done_up.at[s - X], block(out, *spot(w, s)))
    writes.add(w["near_upper"], done_up.at[0], block(out, *spot(w, X)))
    for j, place in enumerate(right_of(w)):
        writes.add(w["d"], done_right.at[j], block(out, *place))
    for j in range(3):
        writes.add(w["d"], done.at[j], block(out, j + 1, w["first"] + j))

    @pl.when(w["d"])
    def _():
        for j in range(3):
            u = diag1[j].astype(BF16)
            two = lower_step(left1[j], a_low[5 + j], u, inv[w["first"] + j])
            done[j] = two * keep[5 + j, 0:1, :]

    @pl.when(w["d_odd"])
    def _():
        for j in range(4):
            low1[1 + j] = lower_step(held[OFF + j], a_low[1 + j], rb[j], inv[w["off"] + j])
        low1[0] = lower_step(held[X], a_low[0], rb[3], inv[w["off"] + 3])

    fill.run(False)
    writes.run(True)
    writes.run(False)


def last_kernel(late, diag1, base2, low1, low1_d, a_low, inv, keep, *refs):
    w = role()
    if late:
        ra, rb, r5, r7, rd, _, out, done, sem = refs
    else:
        (ra, rb, _, out, done, sem), r7, rd = refs, None, None
    writes = Copies(sem)
    for j in range(4):
        writes.add(w["d_late" if late else "d_early"], done.at[j], block(out, *spot(w, j)))
    for s in range(OFF, HELD):
        writes.add(w["f_late" if late else "near_lower"], done.at[s], block(out, *spot(w, s)))
    if not late:
        writes.add(w["near_lower"], done.at[X], block(out, *spot(w, X)))

    class Own:
        def __getitem__(self, s):
            return low1_d[s - X]

    def emit(j, total):
        old = diag1[j]
        done[DIAG + j] = old + (total - old)

    each_diagonal(w, late, emit, base2, Own(), rb, ra, r7, rd)

    def lower(old, u, j, s):
        two = lower_step(old[s - X], a_low[s - X], u[j], inv[w["off"] + j])
        done[s] = two * keep[s - X, 0:1, :]

    for name, old, u in (("f_late", low1, r5),) if late else (("d_odd", low1_d, rb), ("n_even", low1, rb)):

        @pl.when(w[name])
        def _():
            for j in range(4):
                lower(old, u, j, OFF + j)
            if not late:
                lower(old, u, 3, X)

    writes.run(True)
    writes.run(False)


def needed():
    def at(r, c):
        return r * 8 + c

    diag = [at(r, r // 2) for r in range(16)]
    near = {r: at(r, r // 2 + (1 if r % 2 else -1)) for r in range(1, 15)}
    far = [at(r, r // 2 + (4 if r < 8 else -4)) for r in range(16)]
    pair = [(diag[r], diag[r + 1]) for r in range(0, 16, 2)]
    up = [(near[r], diag[r + 1]) for r in range(1, 14, 2)]
    low = [(near[r], diag[r]) for r in range(2, 15, 2)]
    onward = [(diag[r], near[r + 1]) for r in range(1, 14, 2)]
    down = [(diag[r], far[r + 8]) for r in range(8)]
    far_l = [(far[r], diag[r]) for r in range(8, 16)]
    far_u = [(far[r], diag[r + 8]) for r in range(8)]
    return {
        "l": pair + low,
        "u": pair + up + onward,
        "far_l": down + far_l,
        "far_u": far_u,
        "u2": pair + up,
        "far_u2": far_u,
        "l2": pair + low + onward,
        "down": down,
        "far_l2": far_l,
    }


RECEIVERS = {
    "l": [
        8, 41, 10, 11, 12, 13, 31, 15, 9, 1, 2, 3, 4, 5, 6, 7,
        17, 25, 26, 27, 28, 29, 24, 30, 16, 0, 18, 19, 20, 21, 22, 23,
        40, 34, 42, 58, 37, 43, 46, 79, 32, 33, 44, 35, 45, 47, 38, 39,
        88, 56, 51, 59, 60, 61, 62, 63, 48, 49, 50, 57, 52, 53, 54, 55,
        72, 73, 74, 68, 76, 77, 78, 111, 64, 65, 66, 67, 36, 69, 70, 71,
        94, 89, 75, 90, 85, 93, 92, 95, 80, 81, 82, 83, 84, 91, 86, 87,
        104, 105, 106, 107, 108, 102, 110, 126, 96, 97, 98, 99, 100, 101, 14, 103,
        120, 121, 122, 123, 109, 124, 119, 127, 112, 113, 114, 115, 116, 117, 118, 125,
    ],
    "u": [
        8, 9, 10, 11, 12, 13, 0, 15, 16, 17, 2, 3, 4, 5, 6, 7,
        24, 25, 26, 27, 28, 29, 30, 31, 18, 33, 34, 19, 20, 21, 22, 14,
        40, 41, 42, 43, 44, 45, 46, 47, 32, 1, 50, 51, 36, 37, 38, 39,
        56, 57, 58, 59, 60, 61, 62, 63, 48, 49, 52, 67, 68, 53, 54, 55,
        72, 73, 74, 75, 76, 77, 78, 79, 64, 65, 66, 35, 84, 85, 70, 71,
        88, 89, 90, 91, 92, 93, 94, 95, 80, 81, 82, 83, 86, 101, 102, 87,
        104, 105, 106, 107, 108, 109, 110, 111, 96, 97, 98, 99, 100, 69, 118, 119,
        120, 121, 122, 123, 124, 125, 126, 127, 112, 113, 114, 115, 116, 117, 103, 23,
    ],
    "far_l": [
        64, 9, 10, 11, 12, 13, 14, 15, 72, 1, 2, 3, 4, 5, 6, 7,
        24, 81, 26, 27, 28, 29, 30, 25, 16, 89, 18, 19, 20, 21, 22, 17,
        40, 41, 98, 43, 42, 45, 46, 47, 32, 33, 106, 35, 34, 37, 38, 39,
        56, 57, 58, 115, 60, 59, 62, 63, 48, 49, 50, 123, 52, 51, 54, 55,
        68, 73, 74, 75, 36, 77, 78, 79, 76, 65, 66, 67, 44, 69, 70, 71,
        88, 85, 90, 91, 92, 53, 94, 95, 80, 93, 82, 83, 84, 61, 86, 87,
        8, 105, 102, 107, 108, 109, 104, 111, 0, 97, 110, 99, 100, 101, 96, 103,
        120, 121, 122, 119, 124, 125, 126, 23, 112, 113, 114, 127, 116, 117, 118, 31,
    ],
    "far_u": [
        8, 9, 10, 11, 68, 13, 14, 15, 0, 1, 2, 3, 76, 5, 6, 7,
        24, 25, 26, 27, 28, 85, 30, 63, 16, 17, 18, 19, 20, 93, 22, 23,
        40, 41, 42, 43, 44, 45, 102, 47, 32, 33, 34, 35, 38, 37, 110, 39,
        56, 57, 58, 59, 60, 61, 62, 119, 48, 49, 50, 51, 52, 55, 54, 127,
        72, 73, 74, 75, 36, 77, 78, 79, 64, 65, 66, 67, 100, 69, 46, 71,
        88, 89, 90, 91, 92, 117, 94, 95, 80, 81, 82, 83, 84, 53, 86, 87,
        104, 105, 106, 107, 4, 109, 70, 111, 96, 97, 98, 99, 12, 101, 108, 103,
        120, 121, 122, 123, 124, 21, 126, 31, 112, 113, 114, 115, 116, 29, 118, 125,
    ],
    "u2": [
        8, 9, 10, 11, 12, 13, 14, 15, 0, 17, 2, 3, 4, 5, 1, 7,
        24, 25, 26, 27, 28, 29, 30, 31, 16, 19, 34, 18, 20, 21, 22, 6,
        40, 41, 42, 43, 44, 45, 46, 47, 32, 33, 35, 51, 36, 37, 38, 39,
        56, 57, 58, 59, 60, 61, 62, 63, 48, 49, 50, 53, 68, 52, 54, 55,
        72, 73, 74, 75, 76, 77, 78, 79, 64, 65, 66, 67, 69, 85, 70, 71,
        88, 89, 90, 91, 92, 93, 94, 95, 80, 81, 82, 83, 84, 87, 102, 86,
        104, 105, 106, 107, 108, 109, 110, 111, 96, 97, 98, 99, 100, 101, 103, 119,
        120, 121, 122, 123, 124, 125, 126, 127, 112, 113, 114, 115, 116, 117, 118, 23,
    ],
    "far_u2": [
        8, 9, 10, 11, 68, 13, 38, 15, 0, 1, 2, 3, 76, 5, 46, 7,
        24, 25, 26, 27, 28, 85, 30, 63, 16, 17, 18, 19, 20, 93, 22, 55,
        40, 41, 42, 43, 44, 45, 102, 47, 32, 33, 34, 35, 36, 37, 110, 39,
        56, 57, 58, 59, 60, 61, 62, 119, 48, 49, 50, 51, 52, 53, 54, 127,
        72, 73, 74, 75, 100, 77, 78, 79, 64, 65, 66, 67, 108, 69, 70, 71,
        88, 89, 90, 91, 92, 125, 94, 95, 80, 81, 82, 83, 84, 117, 86, 87,
        104, 105, 106, 107, 12, 109, 14, 111, 96, 97, 98, 99, 4, 101, 6, 103,
        120, 121, 122, 123, 124, 21, 126, 23, 112, 113, 114, 115, 116, 29, 118, 31,
    ],
    "l2": [
        8, 9, 10, 11, 12, 13, 14, 15, 16, 1, 2, 3, 4, 5, 6, 7,
        17, 25, 26, 27, 28, 29, 30, 31, 58, 33, 18, 19, 20, 21, 22, 23,
        40, 34, 42, 43, 44, 45, 46, 47, 0, 32, 50, 35, 36, 37, 38, 39,
        56, 57, 51, 59, 60, 61, 62, 63, 48, 49, 92, 67, 52, 53, 54, 55,
        72, 73, 74, 68, 76, 77, 78, 79, 64, 65, 66, 41, 84, 69, 70, 71,
        88, 89, 90, 91, 85, 93, 94, 95, 80, 81, 82, 83, 109, 101, 86, 87,
        104, 105, 106, 107, 108, 102, 110, 111, 96, 97, 98, 99, 100, 75, 118, 103,
        120, 121, 122, 123, 124, 125, 119, 127, 112, 113, 114, 115, 116, 117, 24, 126,
    ],
    "down": [
        64, 9, 42, 11, 12, 13, 14, 15, 72, 1, 34, 3, 4, 5, 6, 7,
        24, 81, 26, 59, 28, 29, 30, 31, 16, 89, 18, 51, 20, 21, 22, 23,
        40, 41, 98, 43, 44, 45, 46, 47, 32, 33, 106, 35, 36, 37, 38, 39,
        56, 57, 58, 115, 60, 61, 62, 63, 48, 49, 50, 123, 52, 53, 54, 55,
        104, 73, 74, 75, 76, 77, 78, 79, 96, 65, 66, 67, 68, 69, 70, 71,
        88, 113, 90, 91, 92, 93, 94, 95, 80, 121, 82, 83, 84, 85, 86, 87,
        0, 105, 10, 107, 108, 109, 110, 111, 8, 97, 2, 99, 100, 101, 102, 103,
        120, 17, 122, 27, 124, 125, 126, 127, 112, 25, 114, 19, 116, 117, 118, 119,
    ],
    "far_l2": [
        8, 9, 10, 11, 12, 13, 14, 15, 0, 1, 2, 3, 4, 5, 6, 7,
        24, 25, 26, 27, 28, 29, 30, 31, 16, 17, 18, 19, 20, 21, 22, 23,
        40, 41, 42, 43, 44, 45, 46, 47, 32, 33, 34, 35, 36, 37, 38, 39,
        56, 57, 58, 59, 60, 61, 62, 63, 48, 49, 50, 51, 52, 53, 54, 55,
        68, 73, 74, 75, 66, 77, 78, 79, 76, 65, 64, 67, 108, 69, 70, 71,
        88, 85, 90, 91, 92, 83, 94, 95, 80, 93, 82, 123, 84, 117, 86, 81,
        98, 105, 102, 107, 106, 109, 104, 111, 72, 97, 110, 99, 100, 101, 96, 103,
        120, 121, 122, 119, 124, 125, 126, 113, 112, 89, 114, 127, 116, 115, 118, 87,
    ],
}


def move(name, buffer):
    return lax.ppermute(buffer, ("row", "col"), ROUTES[name])


ROUTES = {name: list(enumerate(to)) for name, to in RECEIVERS.items()}
for name, pairs in needed().items():
    assert set(pairs) <= set(ROUTES[name]), name
ANY = pl.BlockSpec(memory_space=pl.ANY)
VM = pl.BlockSpec(memory_space=pltpu.VMEM)
MIB = 1 << 20


def wide(n):
    return jax.ShapeDtypeStruct((n, BS, BS), F32)


def half(n):
    return jax.ShapeDtypeStruct((n, BS, BS), BF16)


SENT = [half(5), half(5), half(4), half(4)]
FAR_ROWS, DOWN_ROWS = 6, 6


def call(kernel, name, out_shape, in_specs, out_specs, scratch, aliases=None, cost=None):
    return pl.pallas_call(
        kernel,
        out_shape=out_shape,
        in_specs=in_specs,
        out_specs=out_specs,
        scratch_shapes=scratch,
        input_output_aliases=aliases or {},
        compiler_params=pltpu.CompilerParams(vmem_limit_bytes=20 * MIB),
        cost_estimate=cost and pl.CostEstimate(flops=cost[0], bytes_accessed=cost[1], transcendentals=0),
        name=name,
    )


def on_device(matrix, factors, inverse, pattern, dropped):
    matrix, factors, inverse, pattern, dropped = (
        pltpu.with_memory_space_constraint(x, pltpu.HBM)
        for x in (matrix, factors, inverse, pattern, dropped)
    )
    table = pltpu.SMEM(pattern.shape, jnp.int32)
    sem = pltpu.SemaphoreType.DMA
    whole_out = jax.ShapeDtypeStruct(factors.shape, F32)

    *sent, held = call(
        cut_kernel, "cut", [*SENT, wide(HELD)], [ANY] * 2, [VM] * 5, [table, sem, sem],
    )(pattern, factors)
    rb = move("l", sent[1])
    ra = move("u", sent[0])
    rc = move("far_l", sent[2])
    rd = move("far_u", sent[3])
    upper_b, upper_f, done_up = call(
        upper_kernel,
        "upper",
        [half(6), half(FAR_ROWS), wide(5)],
        [ANY] * 3 + [VM],
        [VM] * 3,
        [pltpu.VMEM((5, BS, BS), BF16), table, table, sem((2,))],
        cost=(10_000_000, 2_000_000),
    )(pattern, dropped, matrix, held)
    ra2 = move("u2", upper_b)
    rd2 = move("far_u2", upper_f)
    base, base2, a_low, left1, inv, keep, done_right = call(
        stage_kernel,
        "stage",
        [wide(4), wide(4), half(8), wide(3), half(inverse.shape[0]),
         jax.ShapeDtypeStruct((8, 8, BS), F32), wide(3)],
        [ANY] * 5 + [VM],
        [VM] * 7,
        [pltpu.VMEM((6, BS, BS), F32), pltpu.VMEM((15, BS, BS), BF16), table, table, sem((4,))],
        cost=(60_000_000, 6_000_000),
    )(pattern, dropped, factors, matrix, inverse, held)
    parts = [half(5), wide(4), wide(5)]
    *part, sent_down = call(
        functools.partial(middle_kernel, False), "early", [*parts, half(DOWN_ROWS)], [VM] * 6, [VM] * 4, [],
    )(held, base, a_low, inv, ra, rb)
    r5 = move("down", sent_down)
    sent_b, diag1, low1, sent_far = call(
        functools.partial(middle_kernel, True), "late", [*parts, half(4)], [VM] * 11, [VM] * 4, [],
        aliases={8: 0, 9: 1, 10: 2},
    )(held, base, a_low, inv, ra, rb, rc, rd, *part)
    rb2 = move("l2", sent_b)
    r7 = move("far_l2", sent_far)
    out, low1_d = call(
        between_kernel,
        "between",
        [whole_out, wide(5)],
        [VM] * 9,
        [ANY, VM],
        [pltpu.VMEM((64, factors.shape[1]), F32), pltpu.VMEM((3, BS, BS), F32), sem((2,))],
        cost=(60_000_000, 4_000_000),
    )(held, diag1, left1, a_low, inv, keep, rb, done_up, done_right)
    state = (diag1, base2, low1, low1_d, a_low, inv, keep, ra2, rb2)
    ends = [pltpu.VMEM((HELD, BS, BS), F32), sem]
    out = call(
        functools.partial(last_kernel, False), "last_early", whole_out, [VM] * 9 + [ANY], ANY, ends, aliases={9: 0},
    )(*state, out)
    return call(
        functools.partial(last_kernel, True), "last_late", whole_out, [VM] * 12 + [ANY], ANY, ends, aliases={12: 0},
    )(*state, r5, r7, rd2, out)


def solution(mesh):
    placed = (
        P("row", "col"),
        P("row", "col"),
        P("col", None, None),
        P("row", "col"),
        P("row", "col"),
    )
    return jax.shard_map(
        on_device, mesh=mesh, in_specs=placed, out_specs=P("row", "col"), check_vma=False
    )
```

time: 25.2 us -> 20.9 us (0.83)
  the two profiles are of different devices: /device:TPU:16 before, /device:TPU:80 now
where the time goes in v2:
time: 20.9 us; the launch traced here: 20.7 us
  waiting for transfers between devices  9.53 us (46%)
  Pallas kernels  7.6 us (36%)
  starting transfers between devices  3.43 us (16%)
    ppermute x9, waiting for transfers between devices, move(): return lax.ppermute(buffer, ('row', 'col'), ROUTES[name])  9.53 us
    ppermute x9, starting transfers between devices, move(): return lax.ppermute(buffer, ('row', 'col'), ROUTES[name])  3.43 us
    pallas_call x1, Pallas kernels, on_device(): call(between_kernel, 'between', [whole_out, wide(5)], [VM] * 9, [ANY, VM]...  2.18 us
    pallas_call x1, Pallas kernels, on_device(): call(stage_kernel, 'stage', [wide(4), wide(4), half(8), wide(3), half(inv...  2.03 us
    pallas_call x1, Pallas kernels, on_device(): call(cut_kernel, 'cut', [*SENT, wide(HELD)], [ANY] * 2, [VM] * 5, [table,...  1.26 us
    pallas_call x1, Pallas kernels, on_device(): call(upper_kernel, 'upper', [half(6), half(FAR_ROWS), wide(5)], [ANY] * 3...  0.95 us
    pallas_call x1, Pallas kernels, on_device(): call(functools.partial(last_kernel, True), 'last_late', whole_out, [VM] *...  0.94 us
  transfers between devices with their start and end apart: 9, of which 5 were waited for; matrix products, arithmetic and copies ran while one was open for 0% of the time, Pallas kernels for 26%

profile of v2, /device:TPU:80, one launch (start us, length us, event | category | flops | bytes accessed | tf_op | source)
XLA Modules:
  0.0 20.7 jit_solution(10744040181885005636)
XLA Ops:
  0.0 1.3 %cut.1 = (bf16[5,128,128]{2,1,0:T(8,128)(2,1)S(1)}, bf16[5,128,128]{2,1,0:T(8,128)(2,1)S(1)}, bf16[4,128,128]{2,1,0:T(8,128)(2,1)S(1)}, bf16[4,128,128]{2,1,0:T(8,128)(2,1)S(1)}, f32[9,128,128]{2,1,0:T(8,128)S(1)}) custom-call(s32[4,8]{1,0:T(4,128)} %pattern.5, f32[512,1024]{1,0:T(8,128)} %factors.3), custom_call_target="tpu_custom_call" | custom-call | tf_op jit(solution)/shard_map/cut/pallas_call | solution.py:587
  1.3 0.1 collective-permute-start
  1.3 2.9 %collective-permute-start.1 = (bf16[5,128,128]{2,1,0:T(8,128)(2,1)S(1)}, bf16[5,128,128]{2,1,0:T(8,128)(2,1)S(1)}, u32[]{:S(2)}, u32[]{:S(2)}) collective-permute-start(bf16[5,128,128]{2,1,0:T(8,128)(2,1)S(1)} %get-tuple-element.35), channel_id=1, source_target_pairs={{0,8},{1,41},{2,10},{3,11},{4,12},{5,13},{6,31},{7,15},{8,9},{9,1}... | collective-permute-start | bytes 491528 | tf_op jit(solution)/shard_map/ppermute | solution.py:541
  4.2 0.0 collective-permute-start.2
  4.2 0.2 collective-permute-start.3
  4.4 0.9 %upper.1 = (bf16[6,128,128]{2,1,0:T(8,128)(2,1)S(1)}, bf16[6,128,128]{2,1,0:T(8,128)(2,1)S(1)}, f32[5,128,128]{2,1,0:T(8,128)S(1)}) custom-call(s32[4,8]{1,0:T(4,128)} %pattern.5, s32[4,8]{1,0:T(4,128)} %dropped.3, bf16[512,1024]{1,0:T(8,128)(2,1)} %matrix.3, f32[9,128,128]{2,1,0:T(8,128)S(1)} %get-tuple-element.30.held), custom_call_target="tpu_custom_call" | custom-call | flops 10000000 | bytes 2000000 | tf_op jit(solution)/shard_map/upper/pallas_call | solution.py:594
  5.4 0.1 collective-permute-start.4
  5.5 2.0 %stage.1 = (f32[4,128,128]{2,1,0:T(8,128)S(1)}, f32[4,128,128]{2,1,0:T(8,128)S(1)}, bf16[8,128,128]{2,1,0:T(8,128)(2,1)S(1)}, f32[3,128,128]{2,1,0:T(8,128)S(1)}...) custom-call(s32[4,8]{1,0:T(4,128)} %pattern.5, s32[4,8]{1,0:T(4,128)} %dropped.3, ...), custom_call_target="tpu_custom_call" | custom-call | flops 60000000 | bytes 6000000 | tf_op jit(solution)/shard_map/stage/pallas_call | solution.py:605
  7.5 1.1 %collective-permute-done.refs_0_ = bf16[5,128,128]{2,1,0:T(8,128)(2,1)S(1)} collective-permute-done((bf16[5,128,128]{2,1,0:T(8,128)(2,1)S(1)}, bf16[5,128,128]{2,1,0:T(8,128)(2,1)S(1)}, u32[]{:S(2)}, u32[]{:S(2)}) %collective-permute-start) | collective-permute-done | bytes 163872 | tf_op jit(solution)/shard_map/ppermute | solution.py:541
  8.6 0.0 collective-permute-start.8
  8.6 0.0 collective-permute-done.1.refs_1_.rb
  8.6 0.1 collective-permute-start.6
  8.7 2.5 %collective-permute-done.2.refs_2_ = bf16[4,128,128]{2,1,0:T(8,128)(2,1)S(1)} collective-permute-done((bf16[4,128,128]{2,1,0:T(8,128)(2,1)S(1)}, bf16[4,128,128]{2,1,0:T(8,128)(2,1)S(1)}, u32[]{:S(2)}, u32[]{:S(2)}) %collective-permute-start.2) | collective-permute-done | bytes 131104 | tf_op jit(solution)/shard_map/ppermute | solution.py:541
  11.1 0.5 %collective-permute-done.3.refs_3_ = bf16[4,128,128]{2,1,0:T(8,128)(2,1)S(1)} collective-permute-done((bf16[4,128,128]{2,1,0:T(8,128)(2,1)S(1)}, bf16[4,128,128]{2,1,0:T(8,128)(2,1)S(1)}, u32[]{:S(2)}, u32[]{:S(2)}) %collective-permute-start.3) | collective-permute-done | bytes 131104 | tf_op jit(solution)/shard_map/ppermute | solution.py:541
  11.7 0.2 %late.1 = (bf16[5,128,128]{2,1,0:T(8,128)(2,1)S(1)}, f32[4,128,128]{2,1,0:T(8,128)S(1)}, f32[5,128,128]{2,1,0:T(8,128)S(1)}, bf16[4,128,128]{2,1,0:T(8,128)(2,1)S(1)}) custom-call(f32[9,128,128]{2,1,0:T(8,128)S(1)} %get-tuple-element.30.held, f32[4,128,128]{2,1,0:T(8,128)S(1)} %get-tuple-element.31.base, ...), custom_call_target="tpu_custom_call", output_to_operand_aliasing={{0}: (8, {}), {1}: (9, {}), {2}: (10, {})} | custom-call | tf_op jit(solution)/shard_map/late/pallas_call | solution.py:620
  11.9 0.1 collective-permute-start.5
  12.0 0.1 collective-permute-start.7
  12.1 2.2 %between.1 = (f32[512,1024]{1,0:T(8,128)}, f32[5,128,128]{2,1,0:T(8,128)S(1)}) custom-call(f32[9,128,128]{2,1,0:T(8,128)S(1)} %get-tuple-element.30.held, f32[4,128,128]{2,1,0:T(8,128)S(1)} %get-tuple-element.41.diag1, f32[3,128,128]{2,1,0:T(8,128)S(1)} %get-tuple-element.44.left1, bf16[8,128,128]{2,1,0:T(8,128)(2,1)S(1)} %get-tuple-element.32.a_low, ...), custom_call_target="tpu_custom_call" | custom-call | flops 60000000 | bytes 4000000 | tf_op jit(solution)/shard_map/between/pallas_call | solution.py:626
  14.3 0.0 collective-permute-done.4.refs_0_
  14.3 5.1 %collective-permute-done.5.refs_1_ = bf16[5,128,128]{2,1,0:T(8,128)(2,1)S(1)} collective-permute-done((bf16[5,128,128]{2,1,0:T(8,128)(2,1)S(1)}, bf16[5,128,128]{2,1,0:T(8,128)(2,1)S(1)}, u32[]{:S(2)}, u32[]{:S(2)}) %collective-permute-start.5) | collective-permute-done | bytes 163872 | tf_op jit(solution)/shard_map/ppermute | solution.py:541
  19.4 0.0 collective-permute-done.8.refs_4_
  19.4 0.3 %collective-permute-done.7.refs_3_ = bf16[4,128,128]{2,1,0:T(8,128)(2,1)S(1)} collective-permute-done((bf16[4,128,128]{2,1,0:T(8,128)(2,1)S(1)}, bf16[4,128,128]{2,1,0:T(8,128)(2,1)S(1)}, u32[]{:S(2)}, u32[]{:S(2)}) %collective-permute-start.7) | collective-permute-done | bytes 131104 | tf_op jit(solution)/shard_map/ppermute | solution.py:541
  19.7 0.0 collective-permute-done.6.refs_2_
  19.7 0.9 %last_late.1 = f32[512,1024]{1,0:T(8,128)} custom-call(f32[4,128,128]{2,1,0:T(8,128)S(1)} %get-tuple-element.41.diag1, f32[4,128,128]{2,1,0:T(8,128)S(1)} %get-tuple-element.42.base2, f32[5,128,128]{2,1,0:T(8,128)S(1)} %get-tuple-element.43.low1, f32[5,128,128]{2,1,0:T(8,128)S(1)} %get-tuple-element.48.low1_d, ...), custom_call_target="tpu_custom_call", output_to_operand_aliasing={{}: (12, {})} | custom-call | tf_op jit(solution)/shard_map/last_late/pallas_call | solution.py:640
  (2 shorter events, 0.0 us)
Async XLA Ops:
  1.3 7.3 %collective-permute-start = (bf16[5,128,128]{2,1,0:T(8,128)(2,1)S(1)}, bf16[5,128,128]{2,1,0:T(8,128)(2,1)S(1)}, u32[]{:S(2)}, u32[]{:S(2)}) collective-permute-start(bf16[5,128,128]{2,1,0:T(8,128)(2,1)S(1)} %get-tuple-element.34), channel_id=1, source_target_pairs={{0,8},{1,9},{2,10},{3,11},{4,12},{5,13},{6,0},{7,15},{8,16},{9,17}... | collective-permute-start | bytes 491528 | tf_op jit(solution)/shard_map/ppermute | solution.py:541
  1.3 7.3 %collective-permute-start.1 = (bf16[5,128,128]{2,1,0:T(8,128)(2,1)S(1)}, bf16[5,128,128]{2,1,0:T(8,128)(2,1)S(1)}, u32[]{:S(2)}, u32[]{:S(2)}) collective-permute-start(bf16[5,128,128]{2,1,0:T(8,128)(2,1)S(1)} %get-tuple-element.35), channel_id=1, source_target_pairs={{0,8},{1,41},{2,10},{3,11},{4,12},{5,13},{6,31},{7,15},{8,9},{9,1}... | collective-permute-start | bytes 491528 | tf_op jit(solution)/shard_map/ppermute | solution.py:541
  4.2 6.9 %collective-permute-start.2 = (bf16[4,128,128]{2,1,0:T(8,128)(2,1)S(1)}, bf16[4,128,128]{2,1,0:T(8,128)(2,1)S(1)}, u32[]{:S(2)}, u32[]{:S(2)}) collective-permute-start(bf16[4,128,128]{2,1,0:T(8,128)(2,1)S(1)} %get-tuple-element.36), channel_id=1, source_target_pairs={{0,64},{1,9},{2,10},{3,11},{4,12},{5,13},{6,14},{7,15},{8,72},{9,1... | collective-permute-start | bytes 393224 | tf_op jit(solution)/shard_map/ppermute | solution.py:541
  4.2 7.4 %collective-permute-start.3 = (bf16[4,128,128]{2,1,0:T(8,128)(2,1)S(1)}, bf16[4,128,128]{2,1,0:T(8,128)(2,1)S(1)}, u32[]{:S(2)}, u32[]{:S(2)}) collective-permute-start(bf16[4,128,128]{2,1,0:T(8,128)(2,1)S(1)} %get-tuple-element.37), channel_id=1, source_target_pairs={{0,8},{1,9},{2,10},{3,11},{4,68},{5,13},{6,14},{7,15},{8,0},{9,1},... | collective-permute-start | bytes 393224 | tf_op jit(solution)/shard_map/ppermute | solution.py:541
  5.4 8.9 %collective-permute-start.4 = (bf16[6,128,128]{2,1,0:T(8,128)(2,1)S(1)}, bf16[6,128,128]{2,1,0:T(8,128)(2,1)S(1)}, u32[]{:S(2)}, u32[]{:S(2)}) collective-permute-start(bf16[6,128,128]{2,1,0:T(8,128)(2,1)S(1)} %get-tuple-element.49), channel_id=1, source_target_pairs={{0,8},{1,9},{2,10},{3,11},{4,12},{5,13},{6,14},{7,15},{8,0},{9,17}... | collective-permute-start | bytes 589832 | tf_op jit(solution)/shard_map/ppermute | solution.py:541
  8.6 10.8 %collective-permute-start.8 = (bf16[6,128,128]{2,1,0:T(8,128)(2,1)S(1)}, bf16[6,128,128]{2,1,0:T(8,128)(2,1)S(1)}, u32[]{:S(2)}, u32[]{:S(2)}) collective-permute-start(bf16[6,128,128]{2,1,0:T(8,128)(2,1)S(1)} %get-tuple-element.53), channel_id=1, source_target_pairs={{0,8},{1,9},{2,10},{3,11},{4,68},{5,13},{6,38},{7,15},{8,0},{9,1},... | collective-permute-start | bytes 589832 | tf_op jit(solution)/shard_map/ppermute | solution.py:541
  8.6 11.1 %collective-permute-start.6 = (bf16[6,128,128]{2,1,0:T(8,128)(2,1)S(1)}, bf16[6,128,128]{2,1,0:T(8,128)(2,1)S(1)}, u32[]{:S(2)}, u32[]{:S(2)}) collective-permute-start(bf16[6,128,128]{2,1,0:T(8,128)(2,1)S(1)} %get-tuple-element.51), channel_id=1, source_target_pairs={{0,64},{1,9},{2,42},{3,11},{4,12},{5,13},{6,14},{7,15},{8,72},{9,1... | collective-permute-start | bytes 589832 | tf_op jit(solution)/shard_map/ppermute | solution.py:541
  11.9 7.5 %collective-permute-start.5 = (bf16[5,128,128]{2,1,0:T(8,128)(2,1)S(1)}, bf16[5,128,128]{2,1,0:T(8,128)(2,1)S(1)}, u32[]{:S(2)}, u32[]{:S(2)}) collective-permute-start(bf16[5,128,128]{2,1,0:T(8,128)(2,1)S(1)} %get-tuple-element.50), channel_id=1, source_target_pairs={{0,8},{1,9},{2,10},{3,11},{4,12},{5,13},{6,14},{7,15},{8,16},{9,1}... | collective-permute-start | bytes 491528 | tf_op jit(solution)/shard_map/ppermute | solution.py:541
  12.0 7.7 %collective-permute-start.7 = (bf16[4,128,128]{2,1,0:T(8,128)(2,1)S(1)}, bf16[4,128,128]{2,1,0:T(8,128)(2,1)S(1)}, u32[]{:S(2)}, u32[]{:S(2)}) collective-permute-start(bf16[4,128,128]{2,1,0:T(8,128)(2,1)S(1)} %get-tuple-element.52), channel_id=1, source_target_pairs={{0,8},{1,9},{2,10},{3,11},{4,12},{5,13},{6,14},{7,15},{8,0},{9,1},... | collective-permute-start | bytes 393224 | tf_op jit(solution)/shard_map/ppermute | solution.py:541

commit v3 on v2

--- a/solution.py
+++ b/solution.py
@@ -396,12 +396,14 @@
     def emit(j, total):
         old = diag1[j]
         done[DIAG + j] = old + (total - old)
+        pltpu.make_async_copy(done.at[j], block(out, *spot(w, j)), sem).start()
 
     each_diagonal(w, late, emit, base2, Own(), rb, ra, r7, rd)
 
     def lower(old, u, j, s):
         two = lower_step(old[s - X], a_low[s - X], u[j], inv[w["off"] + j])
         done[s] = two * keep[s - X, 0:1, :]
+        pltpu.make_async_copy(done.at[s], block(out, *spot(w, s)), sem).start()
 
     for name, old, u in (("f_late", low1, r5),) if late else (("d_odd", low1_d, rb), ("n_even", low1, rb)):
 
@@ -412,7 +414,6 @@
             if not late:
                 lower(old, u, 3, X)
 
-    writes.run(True)
     writes.run(False)
 
 

time: 20.9 us -> 20.9 us (level)
  no operation moved by 1% of the time
where the time goes in v3:
time: 20.9 us; the launch traced here: 20.6 us
  waiting for transfers between devices  9.53 us (46%)
  Pallas kernels  7.55 us (36%)
  starting transfers between devices  3.43 us (16%)
    ppermute x9, waiting for transfers between devices, move(): return lax.ppermute(buffer, ('row', 'col'), ROUTES[name])  9.53 us
    ppermute x9, starting transfers between devices, move(): return lax.ppermute(buffer, ('row', 'col'), ROUTES[name])  3.43 us
    pallas_call x1, Pallas kernels, on_device(): call(between_kernel, 'between', [whole_out, wide(5)], [VM] * 9, [ANY, VM]...  2.18 us
    pallas_call x1, Pallas kernels, on_device(): call(stage_kernel, 'stage', [wide(4), wide(4), half(8), wide(3), half(inv...  2.03 us
    pallas_call x1, Pallas kernels, on_device(): call(cut_kernel, 'cut', [*SENT, wide(HELD)], [ANY] * 2, [VM] * 5, [table,...  1.26 us
    pallas_call x1, Pallas kernels, on_device(): call(upper_kernel, 'upper', [half(6), half(FAR_ROWS), wide(5)], [ANY] * 3...  0.95 us
    pallas_call x1, Pallas kernels, on_device(): call(functools.partial(last_kernel, True), 'last_late', whole_out, [VM] *...  0.89 us
  transfers between devices with their start and end apart: 9, of which 5 were waited for; matrix products, arithmetic and copies ran while one was open for 0% of the time, Pallas kernels for 26%

profile of v3, /device:TPU:80, one launch (start us, length us, event | category | flops | bytes accessed | tf_op | source)
XLA Modules:
  0.0 20.6 jit_solution(15508720673776690261)
XLA Ops:
  0.0 1.3 %cut.1 = (bf16[5,128,128]{2,1,0:T(8,128)(2,1)S(1)}, bf16[5,128,128]{2,1,0:T(8,128)(2,1)S(1)}, bf16[4,128,128]{2,1,0:T(8,128)(2,1)S(1)}, bf16[4,128,128]{2,1,0:T(8,128)(2,1)S(1)}, f32[9,128,128]{2,1,0:T(8,128)S(1)}) custom-call(s32[4,8]{1,0:T(4,128)} %pattern.5, f32[512,1024]{1,0:T(8,128)} %factors.3), custom_call_target="tpu_custom_call" | custom-call | tf_op jit(solution)/shard_map/cut/pallas_call | solution.py:588
  1.3 0.1 collective-permute-start
  1.3 2.9 %collective-permute-start.1 = (bf16[5,128,128]{2,1,0:T(8,128)(2,1)S(1)}, bf16[5,128,128]{2,1,0:T(8,128)(2,1)S(1)}, u32[]{:S(2)}, u32[]{:S(2)}) collective-permute-start(bf16[5,128,128]{2,1,0:T(8,128)(2,1)S(1)} %get-tuple-element.35), channel_id=1, source_target_pairs={{0,8},{1,41},{2,10},{3,11},{4,12},{5,13},{6,31},{7,15},{8,9},{9,1}... | collective-permute-start | bytes 491528 | tf_op jit(solution)/shard_map/ppermute | solution.py:542
  4.2 0.0 collective-permute-start.2
  4.2 0.2 collective-permute-start.3
  4.4 0.9 %upper.1 = (bf16[6,128,128]{2,1,0:T(8,128)(2,1)S(1)}, bf16[6,128,128]{2,1,0:T(8,128)(2,1)S(1)}, f32[5,128,128]{2,1,0:T(8,128)S(1)}) custom-call(s32[4,8]{1,0:T(4,128)} %pattern.5, s32[4,8]{1,0:T(4,128)} %dropped.3, bf16[512,1024]{1,0:T(8,128)(2,1)} %matrix.3, f32[9,128,128]{2,1,0:T(8,128)S(1)} %get-tuple-element.30.held), custom_call_target="tpu_custom_call" | custom-call | flops 10000000 | bytes 2000000 | tf_op jit(solution)/shard_map/upper/pallas_call | solution.py:595
  5.4 0.1 collective-permute-start.4
  5.5 2.0 %stage.1 = (f32[4,128,128]{2,1,0:T(8,128)S(1)}, f32[4,128,128]{2,1,0:T(8,128)S(1)}, bf16[8,128,128]{2,1,0:T(8,128)(2,1)S(1)}, f32[3,128,128]{2,1,0:T(8,128)S(1)}...) custom-call(s32[4,8]{1,0:T(4,128)} %pattern.5, s32[4,8]{1,0:T(4,128)} %dropped.3, ...), custom_call_target="tpu_custom_call" | custom-call | flops 60000000 | bytes 6000000 | tf_op jit(solution)/shard_map/stage/pallas_call | solution.py:606
  7.5 1.1 %collective-permute-done.refs_0_ = bf16[5,128,128]{2,1,0:T(8,128)(2,1)S(1)} collective-permute-done((bf16[5,128,128]{2,1,0:T(8,128)(2,1)S(1)}, bf16[5,128,128]{2,1,0:T(8,128)(2,1)S(1)}, u32[]{:S(2)}, u32[]{:S(2)}) %collective-permute-start) | collective-permute-done | bytes 163872 | tf_op jit(solution)/shard_map/ppermute | solution.py:542
  8.6 0.0 collective-permute-start.8
  8.6 0.0 collective-permute-done.1.refs_1_.rb
  8.6 0.1 collective-permute-start.6
  8.7 2.5 %collective-permute-done.2.refs_2_ = bf16[4,128,128]{2,1,0:T(8,128)(2,1)S(1)} collective-permute-done((bf16[4,128,128]{2,1,0:T(8,128)(2,1)S(1)}, bf16[4,128,128]{2,1,0:T(8,128)(2,1)S(1)}, u32[]{:S(2)}, u32[]{:S(2)}) %collective-permute-start.2) | collective-permute-done | bytes 131104 | tf_op jit(solution)/shard_map/ppermute | solution.py:542
  11.1 0.5 %collective-permute-done.3.refs_3_ = bf16[4,128,128]{2,1,0:T(8,128)(2,1)S(1)} collective-permute-done((bf16[4,128,128]{2,1,0:T(8,128)(2,1)S(1)}, bf16[4,128,128]{2,1,0:T(8,128)(2,1)S(1)}, u32[]{:S(2)}, u32[]{:S(2)}) %collective-permute-start.3) | collective-permute-done | bytes 131104 | tf_op jit(solution)/shard_map/ppermute | solution.py:542
  11.7 0.2 %late.1 = (bf16[5,128,128]{2,1,0:T(8,128)(2,1)S(1)}, f32[4,128,128]{2,1,0:T(8,128)S(1)}, f32[5,128,128]{2,1,0:T(8,128)S(1)}, bf16[4,128,128]{2,1,0:T(8,128)(2,1)S(1)}) custom-call(f32[9,128,128]{2,1,0:T(8,128)S(1)} %get-tuple-element.30.held, f32[4,128,128]{2,1,0:T(8,128)S(1)} %get-tuple-element.31.base, ...), custom_call_target="tpu_custom_call", output_to_operand_aliasing={{0}: (8, {}), {1}: (9, {}), {2}: (10, {})} | custom-call | tf_op jit(solution)/shard_map/late/pallas_call | solution.py:621
  11.9 0.1 collective-permute-start.5
  12.0 0.1 collective-permute-start.7
  12.1 2.2 %between.1 = (f32[512,1024]{1,0:T(8,128)}, f32[5,128,128]{2,1,0:T(8,128)S(1)}) custom-call(f32[9,128,128]{2,1,0:T(8,128)S(1)} %get-tuple-element.30.held, f32[4,128,128]{2,1,0:T(8,128)S(1)} %get-tuple-element.41.diag1, f32[3,128,128]{2,1,0:T(8,128)S(1)} %get-tuple-element.44.left1, bf16[8,128,128]{2,1,0:T(8,128)(2,1)S(1)} %get-tuple-element.32.a_low, ...), custom_call_target="tpu_custom_call" | custom-call | flops 60000000 | bytes 4000000 | tf_op jit(solution)/shard_map/between/pallas_call | solution.py:627
  14.3 0.0 collective-permute-done.4.refs_0_
  14.3 5.1 %collective-permute-done.5.refs_1_ = bf16[5,128,128]{2,1,0:T(8,128)(2,1)S(1)} collective-permute-done((bf16[5,128,128]{2,1,0:T(8,128)(2,1)S(1)}, bf16[5,128,128]{2,1,0:T(8,128)(2,1)S(1)}, u32[]{:S(2)}, u32[]{:S(2)}) %collective-permute-start.5) | collective-permute-done | bytes 163872 | tf_op jit(solution)/shard_map/ppermute | solution.py:542
  19.4 0.0 collective-permute-done.8.refs_4_
  19.4 0.3 %collective-permute-done.7.refs_3_ = bf16[4,128,128]{2,1,0:T(8,128)(2,1)S(1)} collective-permute-done((bf16[4,128,128]{2,1,0:T(8,128)(2,1)S(1)}, bf16[4,128,128]{2,1,0:T(8,128)(2,1)S(1)}, u32[]{:S(2)}, u32[]{:S(2)}) %collective-permute-start.7) | collective-permute-done | bytes 131104 | tf_op jit(solution)/shard_map/ppermute | solution.py:542
  19.7 0.0 collective-permute-done.6.refs_2_
  19.7 0.9 %last_late.1 = f32[512,1024]{1,0:T(8,128)} custom-call(f32[4,128,128]{2,1,0:T(8,128)S(1)} %get-tuple-element.41.diag1, f32[4,128,128]{2,1,0:T(8,128)S(1)} %get-tuple-element.42.base2, f32[5,128,128]{2,1,0:T(8,128)S(1)} %get-tuple-element.43.low1, f32[5,128,128]{2,1,0:T(8,128)S(1)} %get-tuple-element.48.low1_d, ...), custom_call_target="tpu_custom_call", output_to_operand_aliasing={{}: (12, {})} | custom-call | tf_op jit(solution)/shard_map/last_late/pallas_call | solution.py:641
  (2 shorter events, 0.0 us)
Async XLA Ops:
  1.3 7.3 %collective-permute-start = (bf16[5,128,128]{2,1,0:T(8,128)(2,1)S(1)}, bf16[5,128,128]{2,1,0:T(8,128)(2,1)S(1)}, u32[]{:S(2)}, u32[]{:S(2)}) collective-permute-start(bf16[5,128,128]{2,1,0:T(8,128)(2,1)S(1)} %get-tuple-element.34), channel_id=1, source_target_pairs={{0,8},{1,9},{2,10},{3,11},{4,12},{5,13},{6,0},{7,15},{8,16},{9,17}... | collective-permute-start | bytes 491528 | tf_op jit(solution)/shard_map/ppermute | solution.py:542
  1.3 7.3 %collective-permute-start.1 = (bf16[5,128,128]{2,1,0:T(8,128)(2,1)S(1)}, bf16[5,128,128]{2,1,0:T(8,128)(2,1)S(1)}, u32[]{:S(2)}, u32[]{:S(2)}) collective-permute-start(bf16[5,128,128]{2,1,0:T(8,128)(2,1)S(1)} %get-tuple-element.35), channel_id=1, source_target_pairs={{0,8},{1,41},{2,10},{3,11},{4,12},{5,13},{6,31},{7,15},{8,9},{9,1}... | collective-permute-start | bytes 491528 | tf_op jit(solution)/shard_map/ppermute | solution.py:542
  4.2 6.9 %collective-permute-start.2 = (bf16[4,128,128]{2,1,0:T(8,128)(2,1)S(1)}, bf16[4,128,128]{2,1,0:T(8,128)(2,1)S(1)}, u32[]{:S(2)}, u32[]{:S(2)}) collective-permute-start(bf16[4,128,128]{2,1,0:T(8,128)(2,1)S(1)} %get-tuple-element.36), channel_id=1, source_target_pairs={{0,64},{1,9},{2,10},{3,11},{4,12},{5,13},{6,14},{7,15},{8,72},{9,1... | collective-permute-start | bytes 393224 | tf_op jit(solution)/shard_map/ppermute | solution.py:542
  4.2 7.4 %collective-permute-start.3 = (bf16[4,128,128]{2,1,0:T(8,128)(2,1)S(1)}, bf16[4,128,128]{2,1,0:T(8,128)(2,1)S(1)}, u32[]{:S(2)}, u32[]{:S(2)}) collective-permute-start(bf16[4,128,128]{2,1,0:T(8,128)(2,1)S(1)} %get-tuple-element.37), channel_id=1, source_target_pairs={{0,8},{1,9},{2,10},{3,11},{4,68},{5,13},{6,14},{7,15},{8,0},{9,1},... | collective-permute-start | bytes 393224 | tf_op jit(solution)/shard_map/ppermute | solution.py:542
  5.4 8.9 %collective-permute-start.4 = (bf16[6,128,128]{2,1,0:T(8,128)(2,1)S(1)}, bf16[6,128,128]{2,1,0:T(8,128)(2,1)S(1)}, u32[]{:S(2)}, u32[]{:S(2)}) collective-permute-start(bf16[6,128,128]{2,1,0:T(8,128)(2,1)S(1)} %get-tuple-element.49), channel_id=1, source_target_pairs={{0,8},{1,9},{2,10},{3,11},{4,12},{5,13},{6,14},{7,15},{8,0},{9,17}... | collective-permute-start | bytes 589832 | tf_op jit(solution)/shard_map/ppermute | solution.py:542
  8.6 10.8 %collective-permute-start.8 = (bf16[6,128,128]{2,1,0:T(8,128)(2,1)S(1)}, bf16[6,128,128]{2,1,0:T(8,128)(2,1)S(1)}, u32[]{:S(2)}, u32[]{:S(2)}) collective-permute-start(bf16[6,128,128]{2,1,0:T(8,128)(2,1)S(1)} %get-tuple-element.53), channel_id=1, source_target_pairs={{0,8},{1,9},{2,10},{3,11},{4,68},{5,13},{6,38},{7,15},{8,0},{9,1},... | collective-permute-start | bytes 589832 | tf_op jit(solution)/shard_map/ppermute | solution.py:542
  8.6 11.1 %collective-permute-start.6 = (bf16[6,128,128]{2,1,0:T(8,128)(2,1)S(1)}, bf16[6,128,128]{2,1,0:T(8,128)(2,1)S(1)}, u32[]{:S(2)}, u32[]{:S(2)}) collective-permute-start(bf16[6,128,128]{2,1,0:T(8,128)(2,1)S(1)} %get-tuple-element.51), channel_id=1, source_target_pairs={{0,64},{1,9},{2,42},{3,11},{4,12},{5,13},{6,14},{7,15},{8,72},{9,1... | collective-permute-start | bytes 589832 | tf_op jit(solution)/shard_map/ppermute | solution.py:542
  11.9 7.5 %collective-permute-start.5 = (bf16[5,128,128]{2,1,0:T(8,128)(2,1)S(1)}, bf16[5,128,128]{2,1,0:T(8,128)(2,1)S(1)}, u32[]{:S(2)}, u32[]{:S(2)}) collective-permute-start(bf16[5,128,128]{2,1,0:T(8,128)(2,1)S(1)} %get-tuple-element.50), channel_id=1, source_target_pairs={{0,8},{1,9},{2,10},{3,11},{4,12},{5,13},{6,14},{7,15},{8,16},{9,1}... | collective-permute-start | bytes 491528 | tf_op jit(solution)/shard_map/ppermute | solution.py:542
  12.0 7.7 %collective-permute-start.7 = (bf16[4,128,128]{2,1,0:T(8,128)(2,1)S(1)}, bf16[4,128,128]{2,1,0:T(8,128)(2,1)S(1)}, u32[]{:S(2)}, u32[]{:S(2)}) collective-permute-start(bf16[4,128,128]{2,1,0:T(8,128)(2,1)S(1)} %get-tuple-element.52), channel_id=1, source_target_pairs={{0,8},{1,9},{2,10},{3,11},{4,12},{5,13},{6,14},{7,15},{8,0},{9,1},... | collective-permute-start | bytes 393224 | tf_op jit(solution)/shard_map/ppermute | solution.py:542
